TPU v7x, 256 devices: a whole 4x4x8 slice. The times are simulated.
256 devices in a mesh: dp: 8 (over y, z_lo), row: 8 (over z_hi, core), col: 4 (over x).
Axes of the slice: x: 4, y: 4, z: 8 (z_hi: 4, z_lo: 2; z = z_hi * 2 + z_lo), core: 2. Of those that a mesh axis runs over, the one named last changes fastest.
Arguments:
- single: bfloat16 [8, 8, 512, 768], P('dp', 'col', 'row'), may hold values from -6 to 6
- pair_features: bfloat16 [8, 512, 512, 128], P('dp', 'row', 'col'), may hold values from -80 to 80
- key_valid: int32 [8, 512], P('dp'), may hold values from 0 to 1, as said below
- pair_gain: float32 [128], replicated, may hold values from 0.1 to 1.9
- w_query: bfloat16 [768, 768], P(('row', 'col')), may hold values from -0.21875 to 0.21875
- w_key: bfloat16 [768, 768], P(('row', 'col')), may hold values from -0.21875 to 0.21875
- w_value: bfloat16 [768, 768], P(('row', 'col')), may hold values from -0.21875 to 0.21875
- w_out: bfloat16 [768, 768], P(('row', 'col')), may hold values from -0.21875 to 0.21875
- pair_bias_weight: bfloat16 [128, 16], replicated, may hold values from -20 to 20
- out_cotangent: bfloat16 [8, 8, 512, 768], P('dp', 'col', 'row'), may hold values from -0.0390625 to 0.0390625
Outputs:
- attended: bfloat16 [8, 8, 512, 768], P('dp', 'col', 'row')
- grad_query: float32 [768, 768], P(('row', 'col'))
- grad_key: float32 [768, 768], P(('row', 'col'))
- grad_value: float32 [768, 768], P(('row', 'col'))
- grad_out: float32 [768, 768], P(('row', 'col'))
- grad_bias: float32 [128, 16], replicated
Inputs may be any that keep to these rules, and one draw needn't show every extreme that they name: `key_valid`: each row is 1 on a prefix of at least 256 positions and 0 after it.
All inputs are finite; a program needn't handle non-finite values.
Results may differ from a plain program's by a relative error of at most 0.038.
The roundings to bfloat16 on the way count: a program that leaves them out, or rounds other values in their place, can miss the bound.
Values may be sent and summed in bfloat16 or wider, within the bound.
A program may use at most 128 MiB of HBM per device.

v0:
```python
import math

import jax
import jax.numpy as jnp
from jax import lax
from jax.sharding import PartitionSpec as P

NORM_EPSILON = 1e-05
MASKED = -1000000000.0


def normalize_pair(pair_tile, pair_gain):
    values = pair_tile.astype(jnp.float32)
    center = jnp.mean(values, axis=-1, keepdims=True)
    centered = values - center
    variance = jnp.mean(centered * centered, axis=-1, keepdims=True)
    return (centered * lax.rsqrt(variance + NORM_EPSILON) * pair_gain).astype(jnp.bfloat16)


def project(activations, attention_weight_matrix):
    flat = activations.reshape(-1, activations.shape[-1])
    result = jnp.dot(flat, attention_weight_matrix, preferred_element_type=jnp.float32).astype(
        jnp.bfloat16
    )
    return result.reshape(activations.shape[:-1] + (attention_weight_matrix.shape[1],))


def per_device(
    single,
    pair_features,
    key_valid,
    pair_gain,
    w_query,
    w_key,
    w_value,
    w_out,
    pair_bias_weight,
    out_cotangent,
):
    resident_activation_rows = single[0]
    copies = resident_activation_rows.shape[0]
    own_count = resident_activation_rows.shape[1]
    features = resident_activation_rows.shape[2]
    channels = pair_features.shape[3]
    head_count = pair_bias_weight.shape[1]
    head_size = features // head_count
    scaling = 1.0 / math.sqrt(head_size)
    query_count = pair_features.shape[1]
    column_count = pair_features.shape[2]
    full_query, full_key, full_value, full_out = (
        lax.all_gather(w_query, ("row", "col"), axis=0, tiled=True),
        lax.all_gather(w_key, ("row", "col"), axis=0, tiled=True),
        lax.all_gather(w_value, ("row", "col"), axis=0, tiled=True),
        lax.all_gather(w_out, ("row", "col"), axis=0, tiled=True),
    )
    every_acts = lax.all_gather(resident_activation_rows, "row", axis=1, tiled=True)
    key_proj = project(every_acts, full_key)
    value_proj = project(every_acts, full_value)
    token_count = key_proj.shape[1]
    query_heads = project(resident_activation_rows, full_query).reshape(
        copies, own_count, head_count, head_size
    )
    key_heads = key_proj.reshape(copies, token_count, head_count, head_size)
    value_heads = value_proj.reshape(copies, token_count, head_count, head_size)
    normed = normalize_pair(pair_features[0], pair_gain).reshape(
        query_count * column_count, channels
    )
    tile_bias = lax.dot_general(
        pair_bias_weight, normed, (((0,), (1,)), ((), ())), preferred_element_type=jnp.float32
    )
    tile_bias = tile_bias.reshape(head_count, query_count, column_count)
    bias = lax.all_gather(tile_bias, "col", axis=2, tiled=True)
    scores = (
        jnp.einsum("sihd,sjhd->shij", query_heads, key_heads, preferred_element_type=jnp.float32)
        * scaling
        + bias[None]
    )
    scores = jnp.where(key_valid[0][None, None, None, :] == 1, scores, MASKED)
    peak = jnp.max(scores, axis=3, keepdims=True)
    shifted = jnp.exp(scores - peak)
    totals = jnp.sum(shifted, axis=3)
    merged = jnp.einsum(
        "shij,sjhd->sihd",
        shifted.astype(jnp.bfloat16),
        value_heads,
        preferred_element_type=jnp.float32,
    )
    attention = (merged / jnp.transpose(totals, (0, 2, 1))[..., None]).astype(jnp.bfloat16)
    attention_flat = attention.reshape(copies, own_count, features)
    attended = project(attention_flat, full_out)
    cot_flat = out_cotangent[0].reshape(-1, features)
    grad_out_part = lax.dot_general(
        attention_flat.reshape(-1, features),
        cot_flat,
        (((0,), (0,)), ((), ())),
        preferred_element_type=jnp.float32,
    )
    out_grad = lax.dot_general(
        cot_flat, full_out, (((1,), (1,)), ((), ())), preferred_element_type=jnp.float32
    )
    grad_heads = out_grad.astype(jnp.bfloat16).reshape(copies, own_count, head_count, head_size)
    delta = jnp.sum(grad_heads.astype(jnp.float32) * attention.astype(jnp.float32), axis=3)
    probs = shifted / totals[..., None]
    probs_low = probs.astype(jnp.bfloat16)
    prob_grad = jnp.einsum(
        "sihd,sjhd->shij", grad_heads, value_heads, preferred_element_type=jnp.float32
    )
    score_grad = (probs * (prob_grad - jnp.transpose(delta, (0, 2, 1))[..., None])).astype(
        jnp.bfloat16
    )
    query_gradient_total = (
        jnp.einsum("shij,sjhd->sihd", score_grad, key_heads, preferred_element_type=jnp.float32)
        * scaling
    )
    query_gradient_total = query_gradient_total.reshape(copies, own_count, features).astype(
        jnp.bfloat16
    )
    query_gradient_piece = jnp.einsum(
        "gcv,gcq->vq",
        resident_activation_rows,
        query_gradient_total,
        preferred_element_type=jnp.float32,
    )
    key_part = (
        jnp.einsum("shij,sihd->jshd", score_grad, query_heads, preferred_element_type=jnp.float32)
        * scaling
    )
    value_part = jnp.einsum(
        "shij,sihd->jshd", probs_low, grad_heads, preferred_element_type=jnp.float32
    )
    joint_grad = lax.psum_scatter(
        jnp.stack(
            (
                key_part.reshape(own_count * lax.axis_size("row"), copies, features),
                value_part.reshape(own_count * lax.axis_size("row"), copies, features),
            ),
            axis=2,
        ).astype(jnp.bfloat16),
        "row",
        scatter_dimension=0,
        tiled=True,
    ).astype(jnp.float32)
    acts_wide = resident_activation_rows.astype(jnp.float32)
    grad_key_part = jnp.einsum(
        "snd,nse->de", acts_wide, joint_grad[:, :, 0], precision=lax.Precision.HIGHEST
    )
    grad_value_part = jnp.einsum(
        "snd,nse->de", acts_wide, joint_grad[:, :, 1], precision=lax.Precision.HIGHEST
    )
    copy_total = jnp.sum(score_grad.astype(jnp.float32), axis=0)
    bias_grad = lax.psum_scatter(
        copy_total.astype(jnp.bfloat16), "col", scatter_dimension=2, tiled=True
    )
    bias_grad = bias_grad.reshape(head_count, query_count * column_count)
    grad_bias_part = lax.dot_general(
        normed, bias_grad, (((0,), (1,)), ((), ())), preferred_element_type=jnp.float32
    )
    shards = (
        lax.psum_scatter(
            query_gradient_piece.astype(jnp.bfloat16),
            ("row", "col"),
            scatter_dimension=0,
            tiled=True,
        ).astype(jnp.float32),
        lax.psum_scatter(
            grad_key_part.astype(jnp.bfloat16), ("row", "col"), scatter_dimension=0, tiled=True
        ).astype(jnp.float32),
        lax.psum_scatter(
            grad_value_part.astype(jnp.bfloat16), ("row", "col"), scatter_dimension=0, tiled=True
        ).astype(jnp.float32),
        lax.psum_scatter(
            grad_out_part.astype(jnp.bfloat16), ("row", "col"), scatter_dimension=0, tiled=True
        ).astype(jnp.float32),
    )
    results = (
        lax.psum(shards[0].astype(jnp.bfloat16), "dp").astype(jnp.float32),
        lax.psum(shards[1].astype(jnp.bfloat16), "dp").astype(jnp.float32),
        lax.psum(shards[2].astype(jnp.bfloat16), "dp").astype(jnp.float32),
        lax.psum(shards[3].astype(jnp.bfloat16), "dp").astype(jnp.float32),
    )
    grad_bias = lax.psum(grad_bias_part, ("dp", "row", "col"))
    return (attended[None], results[0], results[1], results[2], results[3], grad_bias)


def solution(mesh):
    placed = (
        P("dp", "col", "row", None),
        P("dp", "row", "col", None),
        P("dp", None),
        P(),
        P(("row", "col"), None),
        P(("row", "col"), None),
        P(("row", "col"), None),
        P(("row", "col"), None),
        P(),
        P("dp", "col", "row", None),
    )
    return jax.shard_map(
        per_device,
        mesh=mesh,
        in_specs=placed,
        out_specs=(
            P("dp", "col", "row", None),
            P(("row", "col"), None),
            P(("row", "col"), None),
            P(("row", "col"), None),
            P(("row", "col"), None),
            P(),
        ),
        check_vma=False,
    )
```

profile of v0, /device:TPU:2, one launch (start us, length us, event | category | flops | bytes accessed | tf_op | source)
XLA Modules:
  0.0 853.0 jit_solution(12103049707629180435)
XLA Ops:
  20.1 44.7 %all-gather.16.cloned.1.call-done = bf16[768,768]{1,0:T(8,128)(2,1)} async-done(((bf16[24,768]{1,0:T(8,128)(2,1)}), bf16[768,768]{1,0:T(8,128)(2,1)}) %all-gather.16.cloned.1.call-update) | async-done | bytes 1179664 | tf_op jit(solution)/shard_map/all_gather | solution.py:54
  68.4 48.8 %all-gather.10.cloned.1.call-done = bf16[768,768]{1,0:T(8,128)(2,1)} async-done(((bf16[24,768]{1,0:T(8,128)(2,1)}), bf16[768,768]{1,0:T(8,128)(2,1)}) %all-gather.10.cloned.1.call-update) | async-done | bytes 1179664 | tf_op jit(solution)/shard_map/all_gather | solution.py:51
  120.0 49.8 %all-gather.8.cloned.1.call-done = bf16[768,768]{1,0:T(8,128)(2,1)} async-done(((bf16[24,768]{1,0:T(8,128)(2,1)}), bf16[768,768]{1,0:T(8,128)(2,1)}) %all-gather.8.cloned.1.call-update) | async-done | bytes 1179664 | tf_op jit(solution)/shard_map/all_gather | solution.py:53
  169.8 32.8 %all-gather.18.cloned.1.call-done = bf16[1,2,512,768]{3,2,1,0:T(8,128)(2,1)} async-done(((bf16[1,2,64,768]{3,2,1,0:T(8,128)(2,1)}), bf16[1,2,512,768]{3,2,1,0:T(8,128)(2,1)}) %all-gather.18.cloned.1.call-update) | async-done | bytes 1572880 | tf_op jit(solution)/shard_map/all_gather | solution.py:56
  202.6 4.3 convolution_convert_fusion.1
  211.0 44.1 %all-gather.12.cloned.1.call-done = bf16[768,768]{1,0:T(8,128)(2,1)} async-done(((bf16[24,768]{1,0:T(8,128)(2,1)}), bf16[768,768]{1,0:T(8,128)(2,1)}) %all-gather.12.cloned.1.call-update) | async-done | bytes 1179664 | tf_op jit(solution)/shard_map/all_gather | solution.py:52
  255.1 4.3 convolution_convert_fusion
  263.5 28.4 %all-gather.14.cloned.1.call-done = f32[16,64,512]{2,1,0:T(8,128)} async-done(((f32[16,64,128]{2,1,0:T(8,128)}), f32[16,64,512]{2,1,0:T(8,128)}) %all-gather.14.cloned.1.call-update) | async-done | bytes 2097168 | tf_op jit(solution)/shard_map/all_gather | solution.py:72
  292.0 3.3 fusion.3
  297.2 2.7 fusion.13
  302.5 5.0 multiply_reduce_fusion.1
  307.5 3.6 fusion.55
  322.5 12.5 %copy.76 = bf16[16,64,512]{0,1,2:T(8,128)(2,1)} copy(bf16[16,64,512]{2,1,0:T(8,128)(2,1)S(1)} %copy-done.12) | data formatting | bytes 2097152
  335.0 15.8 %reshape.86 = bf16[512,1024]{1,0:T(8,128)(2,1)} reshape(bf16[512,64,16]{2,1,0:T(8,128)(2,1)} %bitcast.114) | data formatting | bytes 2097152
  350.9 19.1 %reduce-scatter.15.cloned.1.call-done = bf16[64,2,2,768]{3,0,1,2:T(8,128)(2,1)} async-done(((bf16[512,2,2,768]{3,0,1,2:T(8,128)(2,1)}), bf16[64,2,2,768]{3,0,1,2:T(8,128)(2,1)}) %reduce-scatter.15.cloned.1.call-update) | async-done | bytes 393232 | tf_op jit(solution)/shard_map/reduce_scatter | solution.py:131
  378.3 80.3 %reduce-scatter.19.cloned.1.call-done = bf16[24,768]{1,0:T(8,128)(2,1)} async-done(((bf16[768,768]{1,0:T(8,128)(2,1)}), bf16[24,768]{1,0:T(8,128)(2,1)}) %reduce-scatter.19.cloned.1.call-update) | async-done | bytes 36880
  460.2 23.6 %reduce-scatter.25.cloned.1.call-done = bf16[128,1024]{1,0:T(8,128)(2,1)} async-done(((bf16[512,1024]{1,0:T(8,128)(2,1)}), bf16[128,1024]{1,0:T(8,128)(2,1)}) %reduce-scatter.25.cloned.1.call-update) | async-done | bytes 262160
  483.7 3.4 reshape.87
  487.1 89.7 %reduce-scatter.23.cloned.1.call-done = bf16[24,768]{1,0:T(8,128)(2,1)} async-done(((bf16[768,768]{1,0:T(8,128)(2,1)}), bf16[24,768]{1,0:T(8,128)(2,1)}) %reduce-scatter.23.cloned.1.call-update) | async-done | bytes 36880
  578.4 88.4 %reduce-scatter.21.cloned.1.call-done = bf16[24,768]{1,0:T(8,128)(2,1)} async-done(((bf16[768,768]{1,0:T(8,128)(2,1)}), bf16[24,768]{1,0:T(8,128)(2,1)}) %reduce-scatter.21.cloned.1.call-update) | async-done | bytes 36880
  668.4 88.1 %reduce-scatter.17.cloned.1.call-done = bf16[24,768]{1,0:T(8,128)(2,1)} async-done(((bf16[768,768]{1,0:T(8,128)(2,1)}), bf16[24,768]{1,0:T(8,128)(2,1)}) %reduce-scatter.17.cloned.1.call-update) | async-done | bytes 36880 | tf_op jit(solution)/shard_map/reduce_scatter | solution.py:171
  756.6 5.3 fusion.46
  761.8 74.2 %psum.39 = f32[128,16]{0,1:T(8,128)} all-reduce(f32[128,16]{0,1:T(8,128)S(1)} %fusion.46), channel_id=1, replica_groups=mesh['dp'=8,'row'=8,'col'=4] {'dp','row','col'}, use_global_device_ids=true, to_apply=%region_16.17 | all-reduce | flops 2048 | bytes 16384 | tf_op jit(solution)/shard_map/psum | solution.py:181
  836.0 4.0 all-reduce.3.cloned.1.call-done
  (111 shorter events, 62.5 us)
Async XLA Ops:
  7.2 57.6 %copy-start = (bf16[1,2,64,768]{3,2,1,0:T(8,128)(2,1)S(1)}, bf16[1,2,64,768]{3,2,1,0:T(8,128)(2,1)}, u32[]{:S(2)}) copy-start(bf16[1,2,64,768]{3,2,1,0:T(8,128)(2,1)} %param.19) | copy-start | bytes 589828
  7.2 5.7 copy-start.2
  7.2 57.5 %all-gather.16.cloned.1.call-start = ((), (), s32[]{:S(2)}) async-start(), calls=%async_computation.10 | async-start | bytes 1216512 | tf_op jit(solution)/shard_map/all_gather | solution.py:54
  7.9 109.3 %all-gather.10.cloned.1.call-start = ((), (), s32[]{:S(2)}) async-start(), calls=%async_computation.7 | async-start | bytes 1216512 | tf_op jit(solution)/shard_map/all_gather | solution.py:51
  8.7 161.1 %all-gather.8.cloned.1.call-start = ((), (), s32[]{:S(2)}) async-start(), calls=%async_computation.6 | async-start | bytes 1216512 | tf_op jit(solution)/shard_map/all_gather | solution.py:53
  9.4 193.2 %all-gather.18.cloned.1.call-start = ((), (), s32[]{:S(2)}) async-start(), calls=%async_computation.13 | async-start | bytes 1769472 | tf_op jit(solution)/shard_map/all_gather | solution.py:56
  10.0 245.2 %all-gather.12.cloned.1.call-start = ((), (), s32[]{:S(2)}) async-start(), calls=%async_computation.8 | async-start | bytes 1216512 | tf_op jit(solution)/shard_map/all_gather | solution.py:52
  10.6 5.3 copy-start.21
  10.6 281.4 %all-gather.14.cloned.1.call-start = ((), (), s32[]{:S(2)}) async-start(), calls=%async_computation.9 | async-start | bytes 2621440 | tf_op jit(solution)/shard_map/all_gather | solution.py:72
  12.9 5.5 copy-start.16
  20.0 97.3 %copy-start.8 = (bf16[1,2,64,768]{3,2,1,0:T(8,128)(2,1)S(1)}, bf16[1,2,64,768]{3,2,1,0:T(8,128)(2,1)}, u32[]{:S(2)}) copy-start(bf16[1,2,64,768]{3,2,1,0:T(8,128)(2,1)} %param.10) | copy-start | bytes 589828
  20.0 350.0 %reduce-scatter.15.cloned.1.call-start = ((), (), s32[]{:S(2)}) async-start(), calls=%async_computation.11 | async-start | bytes 3538944 | tf_op jit(solution)/shard_map/reduce_scatter | solution.py:131
  291.9 3.3 copy-start.1
  302.5 5.0 copy-start.5
  302.5 5.0 copy-start.11
  316.8 141.8 %reduce-scatter.19.cloned.1.call-start = ((), (), s32[]{:S(2)}) async-start(), calls=%async_computation.14 | async-start | bytes 1216512
  322.5 161.2 %reduce-scatter.25.cloned.1.call-start = ((), (), s32[]{:S(2)}) async-start(), calls=%async_computation.17 | async-start | bytes 1310720
  350.8 225.9 %reduce-scatter.23.cloned.1.call-start = ((), (), s32[]{:S(2)}) async-start(), calls=%async_computation.16 | async-start | bytes 1216512
  372.9 293.9 %reduce-scatter.21.cloned.1.call-start = ((), (), s32[]{:S(2)}) async-start(), calls=%async_computation.15 | async-start | bytes 1216512
  375.0 381.5 %reduce-scatter.17.cloned.1.call-start = ((), (), s32[]{:S(2)}) async-start(), calls=%async_computation.12 | async-start | bytes 1216512 | tf_op jit(solution)/shard_map/reduce_scatter | solution.py:171
  377.2 462.9 %all-reduce.3.cloned.1.call-start = ((), (), s32[]{:S(2)}) async-start(), calls=%async_computation.18 | async-start | bytes 1253376 | tf_op jit(solution)/shard_map/psum | solution.py:176
  378.3 378.2 %copy-start.3 = (bf16[1,64,128,128]{3,2,1,0:T(8,128)(2,1)S(1)}, bf16[1,64,128,128]{3,2,1,0:T(8,128)(2,1)}, u32[]{:S(2)}) copy-start(bf16[1,64,128,128]{3,2,1,0:T(8,128)(2,1)} %param.11) | copy-start | bytes 6291460
  378.3 378.2 %copy-start.17 = (f32[64,128]{1,0:T(8,128)S(1)}, f32[64,128]{1,0:T(8,128)}, u32[]{:S(2)}) copy-start(f32[64,128]{1,0:T(8,128)} %copy-done.16) | copy-start | bytes 98308
  378.3 378.2 %copy-start.18 = (f32[64,128]{1,0:T(8,128)S(1)}, f32[64,128]{1,0:T(8,128)}, u32[]{:S(2)}) copy-start(f32[64,128]{1,0:T(8,128)} %get-tuple-element.28) | copy-start | bytes 98308
  (11 other events, 20.0 us)
Sparse Core Ops, SparseCore 0:
  10.6 54.0 all-gather.15
  67.4 49.8 all-gather.9
  119.9 49.8 all-gather.7
  171.5 31.0 all-gather.17
  205.0 50.0 all-gather.11
  256.8 35.0 all-gather.13
  316.9 53.0 reduce-scatter.14
  373.9 84.6 reduce-scatter.18
  461.1 22.5 reduce-scatter.24
  487.9 88.8 reduce-scatter.22
  581.1 85.6 reduce-scatter.20
  671.0 85.4 reduce-scatter.16
  759.7 80.3 all-reduce.2
where the time goes:
time: 854 us; the launch traced here: 853 us
  waiting for transfers between devices  645 us (76%)
  blocking collectives  74.2 us (9%)
  local copies, waits for them, and re-layouts  64.9 us (8%)
  matrix products  41.6 us (5%)
  between operations  14.2 us (2%)
  other arithmetic  12.4 us (1%)
    unnamed x17, waiting for transfers between devices  285 us
    reduce_scatter x1, waiting for transfers between devices, per_device(): lax.psum_scatter(grad_out_part.astype(jnp.bfloat16), ('row', 'col'), scat...  88.1 us
    psum x1, blocking collectives, per_device(): grad_bias = lax.psum(grad_bias_part, ('dp', 'row', 'col'))  74.2 us
    all_gather x1, waiting for transfers between devices, per_device(): lax.all_gather(w_value, ('row', 'col'), axis=0, tiled=True)  49.8 us
    all_gather x1, waiting for transfers between devices, per_device(): lax.all_gather(w_query, ('row', 'col'), axis=0, tiled=True)  48.8 us
    unnamed x57, local copies, waits for them, and re-layouts  48.8 us
    all_gather x1, waiting for transfers between devices, per_device(): lax.all_gather(w_out, ('row', 'col'), axis=0, tiled=True)  44.7 us
    all_gather x1, waiting for transfers between devices, per_device(): lax.all_gather(w_key, ('row', 'col'), axis=0, tiled=True)  44.1 us
  transfers between devices with their start and end apart: 13, of which 13 were waited for; matrix products, arithmetic and copies ran while one was open for 10% of the time, Pallas kernels for 0%

commit v1 on v0

v1 whole, which is shorter than its diff:
```python
import math

import jax
import jax.numpy as jnp
from jax import lax
from jax.experimental import pallas as pl
from jax.experimental.pallas import tpu as pltpu
from jax.sharding import PartitionSpec as P

NORM_EPSILON = 1e-05
MASKED = -1000000000.0
MESH = pl.DeviceIdType.MESH
F32 = jnp.float32
BF16 = jnp.bfloat16
VMEM_LIMIT = 56 * 1024 * 1024


def place():
    dp, row, col = lax.axis_index("dp"), lax.axis_index("row"), lax.axis_index("col")
    return dp // 2, dp % 2, row // 2, row % 2, col


def device(y, z_lo, z_hi, core, x):
    return (y * 2 + z_lo, z_hi * 2 + core, x)


def greet(peers):
    barrier = pltpu.get_barrier_semaphore()
    for peer in peers:
        pl.semaphore_signal(barrier, inc=1, device_id=peer, device_id_type=MESH)
    pl.semaphore_wait(barrier, len(peers))


class Sender:
    def __init__(self, send_sem, recv_sem):
        self.send_sem, self.recv_sem, self.started = send_sem, recv_sem, []

    def send(self, key, src, dst, peer):
        copy = pltpu.make_async_remote_copy(
            src_ref=src,
            dst_ref=dst,
            send_sem=self.send_sem.at[key],
            recv_sem=self.recv_sem.at[key],
            device_id=peer,
            device_id_type=MESH,
        )
        copy.start()
        self.started.append(copy)
        return copy

    def finish(self):
        for copy in self.started:
            copy.wait_send()


def gather_kernel(w_ref, acts_ref, bias_ref, w_full, acts_full, bias_full, local_sem, send_sem, recv_sem):
    y, z_lo, z_hi, core, x = place()
    row = z_hi * 2 + core
    y_peers = [device((y + d) % 4, z_lo, z_hi, core, x) for d in (1, 2, 3)]
    z_peers = [device(y, z_lo, (z_hi + d) % 4, core, x) for d in (1, 2, 3)]
    x_peers = [device(y, z_lo, z_hi, core, (x + d) % 4) for d in (1, 2, 3)]
    partner = device(y, z_lo, z_hi, 1 - core, x)
    greet(y_peers + z_peers + x_peers + [partner])

    out = Sender(send_sem, recv_sem)
    own_w = pltpu.make_async_copy(w_ref.at[y], w_full.at[y, z_hi, core, x], local_sem.at[0])
    own_acts = pltpu.make_async_copy(acts_ref, acts_full.at[:, row], local_sem.at[1])
    columns = pl.ds(pl.multiple_of(x * 128, 128), 128)
    own_bias = pltpu.make_async_copy(bias_ref, bias_full.at[:, :, columns], local_sem.at[2])
    own_w.start()
    z_copies = [
        out.send(d, w_ref.at[y], w_full.at[y, z_hi, core, x], z_peers[d]) for d in range(3)
    ]
    own_acts.start()
    own_bias.start()
    acts_copies = [
        out.send(34 + d, acts_ref, acts_full.at[:, row], z_peers[d]) for d in range(3)
    ]
    acts_core = [out.send(37, acts_ref, acts_full.at[:, row], partner)]
    bias_copies = [
        out.send(41 + d, bias_ref, bias_full.at[:, :, columns], x_peers[d]) for d in range(3)
    ]

    own_w.wait()
    for copy in z_copies:
        copy.wait_recv()
    line = w_full.at[y, :, core, x]
    x_copies = [out.send(3 + d, line, line, x_peers[d]) for d in range(3)]
    y_copies, core_copies = [], []
    for c in range(4):
        if c > 0:
            x_copies[c - 1].wait_recv()
        line = w_full.at[y, :, core, (x + 4 - c) % 4]
        for e in range(3):
            y_copies.append(out.send(6 + 3 * c + e, line, line, y_peers[e]))
        core_copies.append(out.send(18 + c, line, line, partner))
    for d in range(3):
        acts_copies[d].wait_recv()
        block = acts_full.at[:, ((z_hi + 3 - d) % 4) * 2 + core]
        acts_core.append(out.send(38 + d, block, block, partner))
    for c in range(4):
        for e in range(3):
            y_copies[3 * c + e].wait_recv()
            line = w_full.at[(y + 3 - e) % 4, :, core, (x + 4 - c) % 4]
            core_copies.append(out.send(22 + 3 * c + e, line, line, partner))
    for copy in bias_copies + acts_core + core_copies:
        copy.wait_recv()
    own_acts.wait()
    own_bias.wait()
    out.finish()


def gather(weights, acts, bias):
    any_space = pl.BlockSpec(memory_space=pl.ANY)
    return pl.pallas_call(
        gather_kernel,
        out_shape=(
            jax.ShapeDtypeStruct((4, 4, 2, 4, 24, 768), BF16),
            jax.ShapeDtypeStruct((2, 8, 64, 768), BF16),
            jax.ShapeDtypeStruct((16, 64, 512), F32),
        ),
        in_specs=[any_space] * 3,
        out_specs=[any_space] * 3,
        scratch_shapes=[
            pltpu.SemaphoreType.DMA((3,)),
            pltpu.SemaphoreType.DMA((44,)),
            pltpu.SemaphoreType.DMA((44,)),
        ],
        compiler_params=pltpu.CompilerParams(collective_id=0, has_side_effects=True),
        name="gather",
    )(weights, acts, bias)


def reduce_kernel(
    g_ref, bias_grad_ref, normed_ref, out_ref, bias_out_ref,
    from_core, to_y, from_y, to_x, from_x, to_z, from_z, own, last, from_last,
    bias_in, partial, partial_in, send_sem, recv_sem,
):
    y, z_lo, z_hi, core, x = place()
    z = z_hi * 2 + z_lo
    y_peers = [device((y + d) % 4, z_lo, z_hi, core, x) for d in (1, 2, 3)]
    x_peers = [device(y, z_lo, z_hi, core, (x + d) % 4) for d in (1, 2, 3)]
    z_peers = [device(y, (z + d) % 2, ((z + d) % 8) // 2, core, x) for d in range(1, 8)]
    partner = device(y, z_lo, z_hi, 1 - core, x)
    greet(y_peers + x_peers + z_peers + [partner])

    out = Sender(send_sem, recv_sem)
    order = (1, 2, 3, 0)
    core_copies = {}
    for f in order:
        c = (x + f) % 4
        core_copies[f] = out.send(f, g_ref.at[:, :, 1 - core, c], from_core.at[f], partner)
    bias_copies = [
        out.send(29 + d, bias_grad_ref.at[(x + 1 + d) % 4], bias_in.at[d], x_peers[d])
        for d in range(3)
    ]
    y_copies = {}
    for f in order:
        c = (x + f) % 4
        core_copies[f].wait_recv()
        for d in range(3):
            w = (y + 1 + d) % 4

            def add(k, _, f=f, d=d, w=w, c=c):
                total = g_ref[w, k, core, c].astype(F32) + from_core[f, w, k].astype(F32)
                to_y[d, f, k] = total.astype(BF16)
                return 0

            lax.fori_loop(0, 4, add, 0)
            y_copies[f, d] = out.send(4 + 3 * f + d, to_y.at[d, f], from_y.at[d, f], y_peers[d])

    for copy in bias_copies:
        copy.wait_recv()

    def tile_rows(block, total):
        for u in range(8):
            i = block * 8 + u
            summed = (
                bias_grad_ref[x, i].astype(F32)
                + bias_in[0, i].astype(F32)
                + bias_in[1, i].astype(F32)
                + bias_in[2, i].astype(F32)
            ).astype(BF16)
            total = total + jnp.dot(summed, normed_ref[i], preferred_element_type=F32)
        return total

    partial[0] = lax.fori_loop(0, 8, tile_rows, jnp.zeros((16, 128), F32))
    slot = 0
    for stage, peers in enumerate(([partner], y_peers, x_peers, z_peers)):
        copies = [
            out.send(32 + slot + d, partial.at[stage], partial_in.at[slot + d], peers[d])
            for d in range(len(peers))
        ]
        total = partial[stage]
        for d, copy in enumerate(copies):
            copy.wait_recv()
            total = total + partial_in[slot + d]
        slot += len(peers)
        if stage < 3:
            partial[stage + 1] = total
        else:
            bias_out_ref[...] = total

    x_copies = []
    for f in order:
        c = (x + f) % 4
        for d in range(3):
            y_copies[f, d].wait_recv()

        def add_planes(k, _, f=f, c=c):
            total = (
                g_ref[y, k, core, c].astype(F32)
                + from_core[f, y, k].astype(F32)
                + from_y[0, f, k].astype(F32)
                + from_y[1, f, k].astype(F32)
                + from_y[2, f, k].astype(F32)
            )
            if f > 0:
                to_x[f - 1, k] = total.astype(BF16)
            else:
                own[k] = total
            return 0

        lax.fori_loop(0, 4, add_planes, 0)
        if f > 0:
            x_copies.append(out.send(15 + f, to_x.at[f - 1], from_x.at[f - 1], x_peers[f - 1]))
    for copy in x_copies:
        copy.wait_recv()

    def add_columns(k, _):
        total = (
            own[k]
            + from_x[0, k].astype(F32)
            + from_x[1, k].astype(F32)
            + from_x[2, k].astype(F32)
        )
        own[k] = total
        to_z[k] = total.astype(BF16)
        return 0

    lax.fori_loop(0, 4, add_columns, 0)
    z_copies = []
    for d in range(7):
        target = ((z + 1 + d) % 8) // 2
        z_copies.append(out.send(19 + d, to_z.at[target], from_z.at[d], z_peers[d]))
    for copy in z_copies:
        copy.wait_recv()
    total = own[z_hi]
    for d in range(7):
        total = total + from_z[d].astype(F32)
    last[...] = total
    last_copies = [
        out.send(26 + d, last, from_last.at[d], y_peers[d]) for d in range(3)
    ]
    out_ref[y] = total
    for d, copy in enumerate(last_copies):
        copy.wait_recv()
        out_ref[(y + 3 - d) % 4] = from_last[d]
    out.finish()


def reduce_all(grads, bias_grad, normed):
    vmem = pl.BlockSpec(memory_space=pltpu.VMEM)
    return pl.pallas_call(
        reduce_kernel,
        out_shape=(
            jax.ShapeDtypeStruct((4, 24, 768), F32),
            jax.ShapeDtypeStruct((16, 128), F32),
        ),
        in_specs=[vmem] * 3,
        out_specs=[vmem] * 2,
        scratch_shapes=[
            pltpu.VMEM((4, 4, 4, 24, 768), BF16),
            pltpu.VMEM((3, 4, 4, 24, 768), BF16),
            pltpu.VMEM((3, 4, 4, 24, 768), BF16),
            pltpu.VMEM((3, 4, 24, 768), BF16),
            pltpu.VMEM((3, 4, 24, 768), BF16),
            pltpu.VMEM((4, 24, 768), BF16),
            pltpu.VMEM((7, 24, 768), BF16),
            pltpu.VMEM((4, 24, 768), F32),
            pltpu.VMEM((24, 768), F32),
            pltpu.VMEM((3, 24, 768), F32),
            pltpu.VMEM((3, 64, 16, 128), BF16),
            pltpu.VMEM((4, 16, 128), F32),
            pltpu.VMEM((14, 16, 128), F32),
            pltpu.SemaphoreType.DMA((46,)),
            pltpu.SemaphoreType.DMA((46,)),
        ],
        compiler_params=pltpu.CompilerParams(
            collective_id=1, has_side_effects=True, vmem_limit_bytes=VMEM_LIMIT
        ),
        name="reduce",
    )(grads, bias_grad, normed)


def normalize_pair(pair_tile, pair_gain):
    values = pair_tile.astype(F32)
    center = jnp.mean(values, axis=-1, keepdims=True)
    centered = values - center
    variance = jnp.mean(centered * centered, axis=-1, keepdims=True)
    return (centered * lax.rsqrt(variance + NORM_EPSILON) * pair_gain).astype(BF16)


def project(flat, matrix):
    return jnp.dot(flat, matrix, preferred_element_type=F32).astype(BF16)


def transposed_product(left, right):
    return lax.dot_general(left, right, (((0,), (0,)), ((), ())), preferred_element_type=F32)


def per_device(
    single, pair_features, key_valid, pair_gain, w_query, w_key, w_value, w_out, pair_bias_weight,
    out_cotangent,
):
    own_acts = single[0]
    copies, own_count, features = own_acts.shape
    head_count = 16
    head_size = features // head_count
    scaling = 1.0 / math.sqrt(head_size)
    normed = normalize_pair(pair_features[0], pair_gain)
    tile_bias = lax.dot_general(
        pair_bias_weight, normed, (((0,), (2,)), ((), ())), preferred_element_type=F32
    )
    w_all, acts_all, bias = gather(
        jnp.stack((w_query, w_key, w_value, w_out)), own_acts, tile_bias
    )
    w_all = w_all.reshape(4, features, features)
    token_count = 512
    acts_flat = acts_all.reshape(copies * token_count, features)
    own_flat = own_acts.reshape(copies * own_count, features)
    query = project(own_flat, w_all[0])
    key_proj = project(acts_flat, w_all[1])
    value_proj = project(acts_flat, w_all[2])
    query_heads = query.reshape(copies, own_count, head_count, head_size)
    key_heads = key_proj.reshape(copies, token_count, head_count, head_size)
    value_heads = value_proj.reshape(copies, token_count, head_count, head_size)
    scores = (
        jnp.einsum("sihd,sjhd->shij", query_heads, key_heads, preferred_element_type=F32) * scaling
        + bias[None]
    )
    scores = jnp.where(key_valid[0][None, None, None, :] == 1, scores, MASKED)
    peak = jnp.max(scores, axis=3, keepdims=True)
    shifted = jnp.exp(scores - peak)
    totals = jnp.sum(shifted, axis=3)
    merged = jnp.einsum(
        "shij,sjhd->sihd", shifted.astype(BF16), value_heads, preferred_element_type=F32
    )
    attention = (merged / jnp.transpose(totals, (0, 2, 1))[..., None]).astype(BF16)
    attention_flat = attention.reshape(copies * own_count, features)
    attended = project(attention_flat, w_all[3]).reshape(copies, own_count, features)
    cot_flat = out_cotangent[0].reshape(-1, features)
    grad_out_part = transposed_product(attention_flat, cot_flat)
    out_grad = lax.dot_general(
        cot_flat, w_all[3], (((1,), (1,)), ((), ())), preferred_element_type=F32
    )
    grad_heads = out_grad.astype(BF16).reshape(copies, own_count, head_count, head_size)
    delta = jnp.sum(grad_heads.astype(F32) * attention.astype(F32), axis=3)
    probs = shifted / totals[..., None]
    probs_low = probs.astype(BF16)
    prob_grad = jnp.einsum(
        "sihd,sjhd->shij", grad_heads, value_heads, preferred_element_type=F32
    )
    score_grad = (probs * (prob_grad - jnp.transpose(delta, (0, 2, 1))[..., None])).astype(BF16)
    query_grad = (
        jnp.einsum("shij,sjhd->sihd", score_grad, key_heads, preferred_element_type=F32) * scaling
    )
    query_grad = query_grad.reshape(copies * own_count, features).astype(BF16)
    key_grad = (
        jnp.einsum("shij,sihd->sjhd", score_grad, query_heads, preferred_element_type=F32)
        * scaling
    )
    value_grad = jnp.einsum(
        "shij,sihd->sjhd", probs_low, grad_heads, preferred_element_type=F32
    )
    key_grad = key_grad.reshape(copies * token_count, features).astype(BF16)
    value_grad = value_grad.reshape(copies * token_count, features).astype(BF16)
    grads = jnp.stack(
        (
            transposed_product(own_flat, query_grad).astype(BF16),
            transposed_product(acts_flat, key_grad).astype(BF16),
            transposed_product(acts_flat, value_grad).astype(BF16),
            grad_out_part.astype(BF16),
        )
    ).reshape(4, 4, 2, 4, 24, features)
    bias_grad = jnp.sum(score_grad.astype(F32), axis=0).astype(BF16)
    bias_grad = jnp.transpose(bias_grad.reshape(head_count, own_count, 4, 128), (2, 1, 0, 3))
    results, grad_bias = reduce_all(grads, bias_grad, normed)
    return (attended[None], results[0], results[1], results[2], results[3], grad_bias.T)


def solution(mesh):
    weight = P(("row", "col"), None)
    tokens = P("dp", "col", "row", None)
    return jax.shard_map(
        per_device,
        mesh=mesh,
        in_specs=(
            tokens, P("dp", "row", "col", None), P("dp", None), P(), weight, weight, weight, weight,
            P(), tokens,
        ),
        out_specs=(tokens, weight, weight, weight, weight, P()),
        check_vma=False,
    )
```

time: 854 us -> 207 us (0.24)
  waiting for transfers between devices: 645 us -> 0 us
  Pallas kernels: 0 us -> 127 us
  blocking collectives: 74.2 us -> 0 us
  local copies, waits for them, and re-layouts: 64.9 us -> 35.7 us
  between operations: 14.2 us -> 1.02 us
  matrix products: 41.6 us -> 30.3 us
    unnamed x17 -> x0, waiting for transfers between devices: 285 us -> none
    all_gather x6 -> x0, waiting for transfers between devices: 249 us -> none  [the longest x1 49.8 us: per_device(): lax.all_gather(w_value, ('row', 'col'), axis=0, tiled=True)]
    pallas_call x0 -> x2, Pallas kernels: none -> 127 us  [the longest x1 68.4 us: reduce_all(): pl.pallas_call(reduce_kernel, out_shape=(jax.ShapeDtypeStruct((4, 24, 768...]
    reduce_scatter x2 -> x0, waiting for transfers between devices: 107 us -> none  [the longest x1 88.1 us: per_device(): lax.psum_scatter(grad_out_part.astype(jnp.bfloat16), ('row', 'col'), scat...]
    psum x1 -> x0, blocking collectives: 74.2 us -> none  [per_device(): grad_bias = lax.psum(grad_bias_part, ('dp', 'row', 'col'))]
    unnamed x57 -> x53, local copies, waits for them, and re-layouts: 48.8 us -> 6.95 us
    dot_general x14 -> x13, matrix products: 32.4 us -> 20.7 us  [the longest x4 10 us: project(): return jnp.dot(flat, matrix, preferred_element_type=F32).astype(BF16)]
    another operation x7 -> x0, local copies, waits for them, and re-layouts: 10.5 us -> none  [the longest x2 4.43 us: per_device(): jnp.stack((key_part.reshape(own_count * lax.axis_size('row'), copies, fea...]
  transfers between devices with their start and end apart: 13 -> 0, of which waited for: 13 -> 0; matrix products, arithmetic and copies ran while one was open for 10% -> 0% of each run, Pallas kernels for 0% -> 0%
where the time goes in v1:
time: 207 us
  Pallas kernels  127 us (61%)
  local copies, waits for them, and re-layouts  35.7 us (17%)
  matrix products  30.3 us (15%)
  other arithmetic  12.4 us (6%)
    pallas_call x1, Pallas kernels, reduce_all(): pl.pallas_call(reduce_kernel, out_shape=(jax.ShapeDtypeStruct((4, 24, 768...  68.4 us
    pallas_call x1, Pallas kernels, gather(): pl.pallas_call(gather_kernel, out_shape=(jax.ShapeDtypeStruct((4, 4, 2, 4...  58.9 us
    dot_general x4, matrix products, project(): return jnp.dot(flat, matrix, preferred_element_type=F32).astype(BF16)  10 us
    unnamed x53, local copies, waits for them, and re-layouts  6.95 us
    dot_general x1, matrix products, per_device(): jnp.einsum('sihd,sjhd->shij', grad_heads, value_heads, preferred_element_...  5.38 us
    dot_general x4, matrix products, transposed_product(): lax.dot_general(left, right, (((0,), (0,)), ((), ())), preferred_element_...  4.79 us
    slice x1, local copies, waits for them, and re-layouts, per_device(): w_all[3]  4.18 us

profile of v1, /device:TPU:2, one launch (start us, length us, event | category | flops | bytes accessed | tf_op | source)
XLA Modules:
  0.0 206.7 jit_solution(4897337830912648947)
XLA Ops:
  2.3 2.2 %convert_reduce_fusion = f32[64,128]{1,0:T(8,128)S(1)} fusion(bf16[1,64,128,128]{3,2,1,0:T(8,128)(2,1)} %param.11), kind=kLoop, calls=%fused_computation | loop fusion | flops 2088960 | bytes 2129920 | tf_op jit(solution)/shard_map/reduce_sum | solution.py:298
  4.6 2.4 %fusion.3 = f32[64,128]{1,0:T(8,128)S(1)} fusion(bf16[1,64,128,128]{3,2,1,0:T(8,128)(2,1)S(1)} %copy-done.2, f32[64,128]{1,0:T(8,128)S(1)} %broadcast_multiply_fusion), kind=kLoop, calls=%fused_computation.6 | loop fusion | flops 4186112 | bytes 2162688 | tf_op jit(solution)/shard_map/reduce_sum | solution.py:300
  7.7 2.5 %fusion.5.normed_ref = bf16[64,128,128]{2,1,0:T(8,128)(2,1)S(1)} fusion(bf16[1,64,128,128]{3,2,1,0:T(8,128)(2,1)S(1)} %copy-done.2, f32[128]{0:T(128)S(1)} %copy-done.23, f32[64,128]{1,0:T(8,128)S(1)} %add_rsqrt_fusion, f32[64,128]{1,0:T(8,128)S(1)} %broadcast_multiply_fusion), kind=kLoop, calls=%fused_computation.8 | loop fusion | flops 5242880 | bytes 4260352 | tf_op jit(solution)/shard_map/convert_element_type | solution.py:301
  13.2 58.9 %gather.1 = (bf16[4,4,2,4,24,768]{5,4,3,2,1,0:T(8,128)(2,1)}, bf16[2,8,64,768]{3,2,1,0:T(8,128)(2,1)}, f32[16,64,512]{2,1,0:T(8,128)}) custom-call(bf16[4,24,768]{2,1,0:T(8,128)(2,1)} %pad_maximum_fusion.1.w_ref, bf16[2,64,768]{2,1,0:T(8,128)(2,1)} %bitcast.123, f32[16,64,128]{2,1,0:T(8,128)} %bitcast.122), custom_call_target="tpu_custom_call" | custom-call | tf_op jit(solution)/shard_map/gather/pallas_call | solution.py:115
  72.1 4.2 %fusion.57 = (bf16[1,4,2,4,24,768]{5,4,3,2,1,0:T(8,128)(2,1)S(1)}, bf16[1,4,2,4,24,768]{5,4,3,2,1,0:T(8,128)(2,1)}, bf16[1,4,2,4,24,768]{5,4,3,2,1,0:T(8,128)(2,1)S(1)}, bf16[1,4,2,4,24,768]{5,4,3,2,1,0:T(8,128)(2,1)}) fusion(bf16[4,4,2,4,24,768]{5,4,3,2,1,0:T(8,128)(2,1)} %get-tuple-element.12), kind=kLoop, calls=%fused_computation.63 | loop fusion | bytes 9437184 | tf_op jit(solution)/shard_map/slice | solution.py:351
  79.2 4.3 %convolution_convert_fusion = bf16[1024,768]{1,0:T(8,128)(2,1)} fusion(bf16[1024,768]{1,0:T(8,128)(2,1)} %bitcast.139, bf16[768,768]{1,0:T(8,128)(2,1)} %bitcast.130), kind=kOutput, calls=%fused_computation.20 | convolution fusion | flops 1208745984 | bytes 4325376 | tf_op jit(solution)/shard_map/dot_general | solution.py:305
  83.4 1.7 copy.25
  85.2 2.4 %reshape.88 = bf16[2,512,16,48]{1,0,3,2:T(2,128)(2,1)} reshape(bf16[1024,768]{0,1:T(8,128)(2,1)S(1)} %copy.25) | data formatting | bytes 3145728 | tf_op jit(solution)/shard_map/reshape | solution.py:336
  87.5 3.1 %convolution_convert_fusion.1 = bf16[1024,768]{1,0:T(8,128)(2,1)S(1)} fusion(bf16[1024,768]{1,0:T(8,128)(2,1)} %bitcast.140, bf16[768,768]{1,0:T(8,128)(2,1)} %bitcast.128), kind=kOutput, calls=%fused_computation.21 | convolution fusion | flops 1208745984 | bytes 4325376 | tf_op jit(solution)/shard_map/dot_general | solution.py:305
  90.7 1.7 copy.24
  92.3 4.0 %reshape.86 = bf16[2,512,16,48]{1,0,3,2:T(2,128)(2,1)} reshape(bf16[1024,768]{0,1:T(8,128)(2,1)} %copy.24) | data formatting | bytes 3145728 | tf_op jit(solution)/shard_map/reshape | solution.py:337
  96.4 2.7 %fusion.6 = (f32[2,16,64]{2,1,0:T(8,128)S(1)}, f32[2,16,64,512]{3,2,1,0:T(8,128)S(1)}) fusion(f32[16,64,512]{2,1,0:T(8,128)S(1)} %copy-done.1, pred[512]{0:T(512)(128)(4,1)S(1)} %compare_reduce_fusion, bf16[2,512,16,48]{1,0,3,2:T(2,128)(2,1)} %reshape.88, bf16[2,64,16,48]{1,0,3,2:T(2,128)(2,1)} %reshape.87), kind=kOutput, calls=%fused_computation.12 | convolution fusion | flops 104855552 | bytes 8069632 | tf_op jit(solution)/shard_map/sihd,sjhd->shij/dot_general | solution.py:339
  102.0 1.6 multiply_reduce_fusion
  104.8 1.9 reshape.89
  106.7 2.1 %convolution_convert_fusion.7 = bf16[128,768]{1,0:T(8,128)(2,1)} fusion(bf16[128,768]{0,1:T(8,128)(2,1)} %reshape.89, bf16[768,768]{1,0:T(8,128)(2,1)S(1)} %bitcast.115), kind=kOutput, calls=%fused_computation.41 | convolution fusion | flops 151093248 | bytes 1572864 | tf_op jit(solution)/shard_map/dot_general | solution.py:305
  110.2 5.4 %fusion.58 = (bf16[16,64,512]{2,1,0:T(8,128)(2,1)}, bf16[2,16,64,512]{3,2,1,0:T(8,128)(2,1)S(1)}) fusion(f32[2,16,64]{2,1,0:T(8,128)S(1)} %bitcast.143, bf16[2,512,16,48]{1,0,3,2:T(2,128)(2,1)S(1)} %copy-done.13, bf16[2,64,16,48]{1,0,3,2:T(2,128)(2,1)S(1)} %copy-done.16, f32[2,16,64]{2,1,0:T(8,128)S(1)} %fusion.56, f32[2,16,64]{2,1,0:T(8,128)S(1)} %get-tuple-element.24, ...), kind=kOutput, calls=%fused_computation.64 | convolution fusion | flops 109576192 | bytes 11231744 | tf_op jit(solution)/shard_map/sihd,sjhd->shij/dot_general | solution.py:361
  115.6 2.6 %fusion.14 = bf16[2,512,16,48]{1,3,2,0:T(8,128)(2,1)} fusion(f32[2,16,64]{2,1,0:T(8,128)S(1)} %fusion.56, bf16[2,64,16,48]{1,0,3,2:T(2,128)(2,1)S(1)} %copy-done.16, f32[2,16,64,512]{3,2,1,0:T(8,128)S(1)} %copy-done.5, f32[2,16,64]{2,1,0:T(8,128)S(1)} %get-tuple-element.24, f32[16,64,512]{2,1,0:T(8,128)S(1)} %copy-done.1, ...), kind=kOutput, calls=%fused_computation.26 | convolution fusion | flops 107741184 | bytes 8077824 | tf_op jit(solution)/shard_map/shij,sihd->sjhd/dot_general | solution.py:373
  120.0 1.7 copy.83
  122.3 3.0 %copy.38 = bf16[2,512,16,48]{1,0,3,2:T(2,128)(2,1)S(1)} copy(bf16[2,512,16,48]{1,3,2,0:T(8,128)(2,1)} %fusion.14) | data formatting | bytes 3145728 | tf_op jit(solution)/shard_map/convert_element_type | solution.py:377
  129.3 1.6 copy.36
  131.3 1.5 convolution_convert_fusion.4
  132.8 2.5 %pad_maximum_fusion.g_ref = bf16[4,4,2,4,24,768]{5,4,3,2,1,0:T(8,128)(2,1)} fusion(bf16[1,4,2,4,24,768]{5,4,3,2,1,0:T(8,128)(2,1)S(1)} %bitcast.118, bf16[1,4,2,4,24,768]{5,4,3,2,1,0:T(8,128)(2,1)S(1)} %bitcast.129, bf16[1,4,2,4,24,768]{5,4,3,2,1,0:T(8,128)(2,1)S(1)} %bitcast.131, bf16[1,4,2,4,24,768]{5,4,3,2,1,0:T(8,128)(2,1)S(1)} %bitcast.119), kind=kLoop, calls=%fused_computation.2 | loop fusion | flops 7077888 | bytes 9437184 | tf_op jit(solution)/shard_map/stack | solution.py:378
  135.3 68.4 %reduce.5 = (f32[4,24,768]{2,1,0:T(8,128)}, f32[16,128]{1,0:T(8,128)}) custom-call(bf16[4,4,2,4,24,768]{5,4,3,2,1,0:T(8,128)(2,1)} %pad_maximum_fusion.g_ref, bf16[4,64,16,128]{3,2,1,0:T(8,128)(2,1)} %bitcast.121, bf16[64,128,128]{2,1,0:T(8,128)(2,1)} %copy-done.3), custom_call_target="tpu_custom_call" | custom-call | tf_op jit(solution)/shard_map/reduce/pallas_call | solution.py:264
  203.7 1.7 slice_bitcast_fusion
  (73 shorter events, 21.6 us)
Async XLA Ops:
  0.6 3.9 %copy-start.2 = (bf16[1,64,128,128]{3,2,1,0:T(8,128)(2,1)S(1)}, bf16[1,64,128,128]{3,2,1,0:T(8,128)(2,1)}, u32[]{:S(2)}) copy-start(bf16[1,64,128,128]{3,2,1,0:T(8,128)(2,1)} %param.11) | copy-start | bytes 6291460
  2.3 4.7 %copy-start.18 = (bf16[24,768]{1,0:T(8,128)(2,1)S(1)}, bf16[24,768]{1,0:T(8,128)(2,1)}, u32[]{:S(2)}) copy-start(bf16[24,768]{1,0:T(8,128)(2,1)} %param.17) | copy-start | bytes 110596
  2.3 4.7 %copy-start.19 = (bf16[24,768]{1,0:T(8,128)(2,1)S(1)}, bf16[24,768]{1,0:T(8,128)(2,1)}, u32[]{:S(2)}) copy-start(bf16[24,768]{1,0:T(8,128)(2,1)} %param.16) | copy-start | bytes 110596
  2.3 4.7 %copy-start.20 = (bf16[24,768]{1,0:T(8,128)(2,1)S(1)}, bf16[24,768]{1,0:T(8,128)(2,1)}, u32[]{:S(2)}) copy-start(bf16[24,768]{1,0:T(8,128)(2,1)} %param.15) | copy-start | bytes 110596
  2.3 4.7 %copy-start.21 = (bf16[24,768]{1,0:T(8,128)(2,1)S(1)}, bf16[24,768]{1,0:T(8,128)(2,1)}, u32[]{:S(2)}) copy-start(bf16[24,768]{1,0:T(8,128)(2,1)} %param.14) | copy-start | bytes 110596
  2.3 5.4 %copy-start.23 = (f32[128]{0:T(128)S(1)}, f32[128]{0:T(128)}, u32[]{:S(2)}) copy-start(f32[128]{0:T(128)} %param.13) | copy-start | bytes 1540
  7.7 3.9 %copy-start.22 = (bf16[128,16]{0,1:T(8,128)(2,1)S(1)}, bf16[128,16]{0,1:T(8,128)(2,1)}, u32[]{:S(2)}) copy-start(bf16[128,16]{0,1:T(8,128)(2,1)} %param.18) | copy-start | bytes 12292
  10.2 1.4 copy-start.3
  76.3 1.4 copy-start.10
  92.3 4.0 %copy-start.1 = (f32[16,64,512]{2,1,0:T(8,128)S(1)}, f32[16,64,512]{2,1,0:T(8,128)}, u32[]{:S(2)}) copy-start(f32[16,64,512]{2,1,0:T(8,128)} %get-tuple-element.13) | copy-start | bytes 6291460
  99.1 2.1 %copy-start.4 = (f32[2,16,64,512]{3,2,1,0:T(8,128)}, f32[2,16,64,512]{3,2,1,0:T(8,128)S(1)}, u32[]{:S(2)}) copy-start(f32[2,16,64,512]{3,2,1,0:T(8,128)S(1)} %get-tuple-element.25) | copy-start | bytes 12582916
  99.1 2.6 %copy-start.12 = (bf16[2,512,16,48]{1,0,3,2:T(2,128)(2,1)S(1)}, bf16[2,512,16,48]{1,0,3,2:T(2,128)(2,1)}, u32[]{:S(2)}) copy-start(bf16[2,512,16,48]{1,0,3,2:T(2,128)(2,1)} %reshape.86) | copy-start | bytes 4718596
  99.1 2.9 %copy-start.15 = (bf16[2,64,16,48]{1,0,3,2:T(2,128)(2,1)S(1)}, bf16[2,64,16,48]{1,0,3,2:T(2,128)(2,1)}, u32[]{:S(2)}) copy-start(bf16[2,64,16,48]{1,0,3,2:T(2,128)(2,1)} %reshape.90) | copy-start | bytes 589828
  106.7 3.5 %copy-start.13 = (bf16[2,512,16,48]{1,0,3,2:T(2,128)(2,1)S(1)}, bf16[2,512,16,48]{1,0,3,2:T(2,128)(2,1)}, u32[]{:S(2)}) copy-start(bf16[2,512,16,48]{1,0,3,2:T(2,128)(2,1)} %reshape.86) | copy-start | bytes 4718596
  106.7 3.5 %copy-start.16 = (bf16[2,64,16,48]{1,0,3,2:T(2,128)(2,1)S(1)}, bf16[2,64,16,48]{1,0,3,2:T(2,128)(2,1)}, u32[]{:S(2)}) copy-start(bf16[2,64,16,48]{1,0,3,2:T(2,128)(2,1)} %reshape.90) | copy-start | bytes 589828
  110.2 5.4 %copy-start.5 = (f32[2,16,64,512]{3,2,1,0:T(8,128)S(1)}, f32[2,16,64,512]{3,2,1,0:T(8,128)}, u32[]{:S(2)}) copy-start(f32[2,16,64,512]{3,2,1,0:T(8,128)} %copy-done.4) | copy-start | bytes 12582916
  115.6 2.6 %copy-start.8 = (bf16[2,16,64,512]{3,2,1,0:T(8,128)(2,1)}, bf16[2,16,64,512]{3,2,1,0:T(8,128)(2,1)S(1)}, u32[]{:S(2)}) copy-start(bf16[2,16,64,512]{3,2,1,0:T(8,128)(2,1)S(1)} %get-tuple-element.29) | copy-start | bytes 6291460
  115.6 2.6 %copy-start.6 = (bf16[2,512,16,48]{1,0,3,2:T(2,128)(2,1)S(1)}, bf16[2,512,16,48]{1,0,3,2:T(2,128)(2,1)}, u32[]{:S(2)}) copy-start(bf16[2,512,16,48]{1,0,3,2:T(2,128)(2,1)} %reshape.88) | copy-start | bytes 4718596
  118.3 1.5 copy-start.14
  120.0 1.7 copy-start.17
  125.3 1.4 copy-start.24
  126.7 1.5 copy-start.11
  126.7 2.0 copy-start.7
  126.7 2.0 copy-start.9
  (1 other events, 0.9 us)

commit v2 on v1

v2 whole, which is shorter than its diff:
```python
import math

import jax
import jax.numpy as jnp
from jax import lax
from jax.experimental import pallas as pl
from jax.experimental.pallas import tpu as pltpu
from jax.sharding import PartitionSpec as P

NORM_EPSILON = 1e-05
MASKED = -1000000000.0
MESH = pl.DeviceIdType.MESH
F32 = jnp.float32
BF16 = jnp.bfloat16
VMEM_LIMIT = 56 * 1024 * 1024


def place():
    dp, row, col = lax.axis_index("dp"), lax.axis_index("row"), lax.axis_index("col")
    return dp // 2, dp % 2, row // 2, row % 2, col


def device(y, z_lo, z_hi, core, x):
    return (y * 2 + z_lo, z_hi * 2 + core, x)


def greet(peers):
    barrier = pltpu.get_barrier_semaphore()
    for peer in peers:
        pl.semaphore_signal(barrier, inc=1, device_id=peer, device_id_type=MESH)
    pl.semaphore_wait(barrier, len(peers))


class Sender:
    def __init__(self, send_sem, recv_sem):
        self.send_sem, self.recv_sem, self.started = send_sem, recv_sem, []

    def send(self, src, dst, peer):
        key = len(self.started)
        copy = pltpu.make_async_remote_copy(
            src_ref=src,
            dst_ref=dst,
            send_sem=self.send_sem.at[key],
            recv_sem=self.recv_sem.at[key],
            device_id=peer,
            device_id_type=MESH,
        )
        copy.start()
        self.started.append(copy)
        return copy

    def finish(self):
        for copy in self.started:
            copy.wait_send()


def gather_kernel(
    w_ref, acts_ref, pair_ref, gain_ref, pair_weight_ref,
    w_full, acts_full, bias_full, normed_ref,
    tile_bias, local_sem, send_sem, recv_sem,
):
    y, z_lo, z_hi, core, x = place()
    row = z_hi * 2 + core
    y_next, y_back = [device((y + d) % 4, z_lo, z_hi, core, x) for d in (1, 3)]
    x_next, x_back = [device(y, z_lo, z_hi, core, (x + d) % 4) for d in (1, 3)]
    z_peers = [device(y, z_lo, (z_hi + d) % 4, core, x) for d in (1, 2, 3)]
    z_next, z_back = z_peers[0], z_peers[2]
    partner = device(y, z_lo, z_hi, 1 - core, x)
    greet([y_next, y_back, x_next, x_back, partner] + z_peers)

    def normalize_rows(block):
        def one_row(k, _):
            i = block * 16 + k
            values = pair_ref[i].astype(F32)
            center = jnp.mean(values, axis=-1, keepdims=True)
            centered = values - center
            variance = jnp.mean(centered * centered, axis=-1, keepdims=True)
            normed = (
                centered * lax.rsqrt(variance + NORM_EPSILON) * gain_ref[...]
            ).astype(BF16)
            normed_ref[i] = normed
            tile_bias[:, i, :] = lax.dot_general(
                pair_weight_ref[...], normed, (((1,), (1,)), ((), ())),
                preferred_element_type=F32,
            )
            return 0

        lax.fori_loop(0, 16, one_row, 0, unroll=4)

    def columns(owner):
        return pl.ds(pl.multiple_of((owner % 4) * 128, 128), 128)

    def line(plane, owner, part=slice(0, 4)):
        return w_full.at[plane % 4, part, core, owner % 4]

    def rows(z_owner):
        return acts_full.at[:, (z_owner % 4) * 2 + core]

    out = Sender(send_sem, recv_sem)
    send = out.send
    first, second = slice(0, 2), slice(2, 4)
    own_w = pltpu.make_async_copy(w_ref.at[y], w_full.at[y, z_hi, core, x], local_sem.at[0])
    own_acts = pltpu.make_async_copy(acts_ref, acts_full.at[:, row], local_sem.at[1])
    own_w.start()
    z_copies = [send(w_ref.at[y], w_full.at[y, z_hi, core, x], peer) for peer in z_peers]
    own_acts.start()
    acts_up = send(acts_ref, rows(z_hi), z_next)
    acts_down = send(acts_ref, rows(z_hi), z_back)
    core_copies = [send(acts_ref, rows(z_hi), partner)]
    normalize_rows(0)

    def swap_planes(owner):
        own = line(y, owner)
        core_copies.append(send(own, own, partner))
        return send(own, own, y_next), send(own, own, y_back)

    own_w.wait()
    for copy in z_copies:
        copy.wait_recv()
    own = line(y, x)
    x_up = send(own, own, x_next)
    x_down = send(own, own, x_back)
    planes = [swap_planes(x)]
    normalize_rows(1)
    x_up.wait_recv()
    part = line(y, x + 3, first)
    x_far_up = send(part, part, x_next)
    x_down.wait_recv()
    part = line(y, x + 1, second)
    x_far_down = send(part, part, x_back)
    planes.append(swap_planes(x + 3))
    planes.append(swap_planes(x + 1))
    acts_up.wait_recv()
    part = acts_full.at[0, ((z_hi + 3) % 4) * 2 + core]
    acts_far_up = send(part, part, z_next)
    acts_down.wait_recv()
    part = acts_full.at[1, ((z_hi + 1) % 4) * 2 + core]
    acts_far_down = send(part, part, z_back)
    core_copies.append(send(rows(z_hi + 3), rows(z_hi + 3), partner))
    core_copies.append(send(rows(z_hi + 1), rows(z_hi + 1), partner))
    x_far_up.wait_recv()
    x_far_down.wait_recv()
    planes.append(swap_planes(x + 2))
    owners = (x, x + 3, x + 1, x + 2)
    far = []

    def relay_planes(n):
        up, down = planes[n]
        owner = owners[n]
        up.wait_recv()
        part = line(y + 3, owner, first)
        far_up = send(part, part, y_next)
        down.wait_recv()
        part = line(y + 1, owner, second)
        far.append((far_up, send(part, part, y_back)))
        for plane in (y + 3, y + 1):
            whole = line(plane, owner)
            core_copies.append(send(whole, whole, partner))

    relay_planes(0)
    normalize_rows(2)
    relay_planes(1)
    normalize_rows(3)
    own_bias = pltpu.make_async_copy(tile_bias, bias_full.at[:, :, columns(x)], local_sem.at[2])
    own_bias.start()
    bias_up = send(tile_bias, bias_full.at[:, :, columns(x)], x_next)
    bias_down = send(tile_bias, bias_full.at[:, :, columns(x)], x_back)
    relay_planes(2)
    relay_planes(3)
    acts_far_up.wait_recv()
    acts_far_down.wait_recv()
    core_copies.append(send(rows(z_hi + 2), rows(z_hi + 2), partner))
    for n in range(4):
        for copy in far[n]:
            copy.wait_recv()
        whole = line(y + 2, owners[n])
        core_copies.append(send(whole, whole, partner))
        if n == 1:
            bias_up.wait_recv()
            part = bias_full.at[slice(0, 8), :, columns(x + 3)]
            bias_far_up = send(part, part, x_next)
            bias_down.wait_recv()
            part = bias_full.at[slice(8, 16), :, columns(x + 1)]
            bias_far_down = send(part, part, x_back)
    for copy in core_copies + [bias_far_up, bias_far_down]:
        copy.wait_recv()
    own_acts.wait()
    own_bias.wait()
    out.finish()


def gather(weights, acts, pair_tile, pair_gain, pair_weight):
    any_space = pl.BlockSpec(memory_space=pl.ANY)
    vmem = pl.BlockSpec(memory_space=pltpu.VMEM)
    return pl.pallas_call(
        gather_kernel,
        out_shape=(
            jax.ShapeDtypeStruct((4, 4, 2, 4, 24, 768), BF16),
            jax.ShapeDtypeStruct((2, 8, 64, 768), BF16),
            jax.ShapeDtypeStruct((16, 64, 512), F32),
            jax.ShapeDtypeStruct((64, 128, 128), BF16),
        ),
        in_specs=[any_space, any_space, vmem, vmem, vmem],
        out_specs=[any_space, any_space, any_space, vmem],
        scratch_shapes=[
            pltpu.VMEM((16, 64, 128), F32),
            pltpu.SemaphoreType.DMA((3,)),
            pltpu.SemaphoreType.DMA((56,)),
            pltpu.SemaphoreType.DMA((56,)),
        ],
        compiler_params=pltpu.CompilerParams(
            collective_id=0, has_side_effects=True, vmem_limit_bytes=VMEM_LIMIT
        ),
        name="gather",
    )(weights, acts, pair_tile, pair_gain, pair_weight)


def reduce_kernel(
    g_ref, bias_grad_ref, normed_ref, out_ref, bias_out_ref,
    from_core, to_far, from_far, to_y, from_y, to_x, from_x, x_halves, to_z, from_z,
    own, last, from_last,
    bias_halves, bias_sent, bias_in, bias_sum, partial, partial_in, send_sem, recv_sem,
):
    y, z_lo, z_hi, core, x = place()
    z = z_hi * 2 + z_lo
    y_peers = [device((y + d) % 4, z_lo, z_hi, core, x) for d in (1, 2, 3)]
    x_peers = [device(y, z_lo, z_hi, core, (x + d) % 4) for d in (1, 2, 3)]
    z_peers = [device(y, (z + d) % 2, ((z + d) % 8) // 2, core, x) for d in range(1, 8)]
    partner = device(y, z_lo, z_hi, 1 - core, x)
    y_next, y_back, x_next, x_back = y_peers[0], y_peers[2], x_peers[0], x_peers[2]
    greet(y_peers + x_peers + z_peers + [partner])

    out = Sender(send_sem, recv_sem)
    send = out.send
    first, second = slice(0, 2), slice(2, 4)
    order = (2, 1, 3, 0)
    core_copies = {}
    for f in order:
        core_copies[f] = send(g_ref.at[:, :, 1 - core, (x + f) % 4], from_core.at[f], partner)
    far_block = bias_grad_ref.at[(x + 2) % 4]
    bias_far = [
        send(far_block.at[slice(0, 8)], bias_halves.at[0], x_next),
        send(far_block.at[slice(8, 16)], bias_halves.at[1], x_back),
    ]

    def both_cores(f, w, k):
        return g_ref[w, k, core, (x + f) % 4].astype(F32) + from_core[f, w, k].astype(F32)

    far, near = {}, {}

    def start_chunk(f):
        core_copies[f].wait_recv()

        def add(k, _):
            to_far[f, k] = both_cores(f, (y + 2) % 4, k).astype(BF16)
            return 0

        lax.fori_loop(0, 4, add, 0)
        far[f] = (
            send(to_far.at[f, first], from_far.at[0, f], y_next),
            send(to_far.at[f, second], from_far.at[1, f], y_back),
        )

    def pass_chunk(f):
        far[f][0].wait_recv()
        far[f][1].wait_recv()

        def add(k, _):
            up, down = (y + 1) % 4, (y + 3) % 4
            to_y[0, f, k] = (
                both_cores(f, up, k) + from_far[0, f, k].astype(F32)
            ).astype(BF16)
            to_y[0, f, k + 2] = both_cores(f, up, k + 2).astype(BF16)
            to_y[1, f, k] = both_cores(f, down, k).astype(BF16)
            to_y[1, f, k + 2] = (
                both_cores(f, down, k + 2) + from_far[1, f, k].astype(F32)
            ).astype(BF16)
            return 0

        lax.fori_loop(0, 2, add, 0)
        near[f] = (
            send(to_y.at[0, f], from_y.at[0, f], y_next),
            send(to_y.at[1, f], from_y.at[1, f], y_back),
        )

    start_chunk(2)
    start_chunk(1)
    pass_chunk(2)
    start_chunk(3)
    pass_chunk(1)
    start_chunk(0)
    for copy in bias_far:
        copy.wait_recv()

    def add_bias(h, _):
        up, down = (x + 1) % 4, (x + 3) % 4
        bias_sent[0, h] = (
            bias_grad_ref[up, h].astype(F32) + bias_halves[0, h].astype(F32)
        ).astype(BF16)
        bias_sent[0, h + 8] = bias_grad_ref[up, h + 8]
        bias_sent[1, h] = bias_grad_ref[down, h]
        bias_sent[1, h + 8] = (
            bias_grad_ref[down, h + 8].astype(F32) + bias_halves[1, h].astype(F32)
        ).astype(BF16)
        return 0

    lax.fori_loop(0, 8, add_bias, 0)
    bias_near = [
        send(bias_sent.at[0], bias_in.at[0], x_next),
        send(bias_sent.at[1], bias_in.at[1], x_back),
    ]
    pass_chunk(3)
    pass_chunk(0)

    for copy in bias_near:
        copy.wait_recv()

    def sum_bias(h, _):
        summed = (
            bias_grad_ref[x, h].astype(F32)
            + bias_in[0, h].astype(F32)
            + bias_in[1, h].astype(F32)
        )
        bias_sum[h] = summed.astype(BF16).astype(F32)
        return 0

    lax.fori_loop(0, 16, sum_bias, 0)

    def tile_rows(block, total):
        for u in range(8):
            i = block * 8 + u
            total = total + jnp.dot(
                bias_sum[:, i, :].astype(BF16), normed_ref[i], preferred_element_type=F32
            )
        return total

    partial[0] = lax.fori_loop(0, 8, tile_rows, jnp.zeros((16, 128), F32))
    stages = ([partner], y_peers, x_peers, z_peers)
    starts = (0, 1, 4, 7)
    in_flight = {}

    def start_stage(n):
        in_flight[n] = [
            send(partial.at[n], partial_in.at[starts[n] + d], peer)
            for d, peer in enumerate(stages[n])
        ]

    def end_stage(n):
        total = partial[n]
        for d, copy in enumerate(in_flight[n]):
            copy.wait_recv()
            total = total + partial_in[starts[n] + d]
        if n < 3:
            partial[n + 1] = total
            start_stage(n + 1)
        else:
            bias_out_ref[...] = total

    def all_planes(f, k):
        return (
            both_cores(f, y, k) + from_y[0, f, k].astype(F32) + from_y[1, f, k].astype(F32)
        )

    def wait_planes(f):
        near[f][0].wait_recv()
        near[f][1].wait_recv()

    start_stage(0)
    wait_planes(2)

    def add_far(k, _):
        to_x[2, k] = all_planes(2, k).astype(BF16)
        return 0

    lax.fori_loop(0, 4, add_far, 0)
    x_far = [
        send(to_x.at[2, first], x_halves.at[0], x_next),
        send(to_x.at[2, second], x_halves.at[1], x_back),
    ]
    end_stage(0)
    wait_planes(1)
    x_far[0].wait_recv()

    def add_up(k, _):
        to_x[0, k] = (all_planes(1, k) + x_halves[0, k].astype(F32)).astype(BF16)
        to_x[0, k + 2] = all_planes(1, k + 2).astype(BF16)
        return 0

    lax.fori_loop(0, 2, add_up, 0)
    x_up = send(to_x.at[0], from_x.at[0], x_next)
    end_stage(1)
    wait_planes(3)
    x_far[1].wait_recv()

    def add_down(k, _):
        to_x[1, k] = all_planes(3, k).astype(BF16)
        to_x[1, k + 2] = (all_planes(3, k + 2) + x_halves[1, k].astype(F32)).astype(BF16)
        return 0

    lax.fori_loop(0, 2, add_down, 0)
    x_down = send(to_x.at[1], from_x.at[1], x_back)
    end_stage(2)
    wait_planes(0)
    x_up.wait_recv()
    x_down.wait_recv()

    def add_own(k, _):
        total = all_planes(0, k) + from_x[0, k].astype(F32) + from_x[1, k].astype(F32)
        own[k] = total
        to_z[k] = total.astype(BF16)
        return 0

    lax.fori_loop(0, 4, add_own, 0)
    z_copies = []
    for d in range(7):
        target = ((z + 1 + d) % 8) // 2
        z_copies.append(send(to_z.at[target], from_z.at[d], z_peers[d]))
    end_stage(3)
    total = own[z_hi]
    for d, copy in enumerate(z_copies):
        copy.wait_recv()
        total = total + from_z[d].astype(F32)
    last[...] = total.astype(BF16)
    last_copies = [send(last, from_last.at[d], y_peers[d]) for d in range(3)]
    out_ref[y] = total.astype(BF16).astype(F32)
    for d, copy in enumerate(last_copies):
        copy.wait_recv()
        out_ref[(y + 3 - d) % 4] = from_last[d].astype(F32)
    out.finish()


def reduce_all(grads, bias_grad, normed):
    vmem = pl.BlockSpec(memory_space=pltpu.VMEM)
    return pl.pallas_call(
        reduce_kernel,
        out_shape=(
            jax.ShapeDtypeStruct((4, 24, 768), F32),
            jax.ShapeDtypeStruct((16, 128), F32),
        ),
        in_specs=[vmem] * 3,
        out_specs=[vmem] * 2,
        scratch_shapes=[
            pltpu.VMEM((4, 4, 4, 24, 768), BF16),
            pltpu.VMEM((4, 4, 24, 768), BF16),
            pltpu.VMEM((2, 4, 2, 24, 768), BF16),
            pltpu.VMEM((2, 4, 4, 24, 768), BF16),
            pltpu.VMEM((2, 4, 4, 24, 768), BF16),
            pltpu.VMEM((3, 4, 24, 768), BF16),
            pltpu.VMEM((2, 4, 24, 768), BF16),
            pltpu.VMEM((2, 2, 24, 768), BF16),
            pltpu.VMEM((4, 24, 768), BF16),
            pltpu.VMEM((7, 24, 768), BF16),
            pltpu.VMEM((4, 24, 768), F32),
            pltpu.VMEM((24, 768), BF16),
            pltpu.VMEM((3, 24, 768), BF16),
            pltpu.VMEM((2, 8, 64, 128), BF16),
            pltpu.VMEM((2, 16, 64, 128), BF16),
            pltpu.VMEM((2, 16, 64, 128), BF16),
            pltpu.VMEM((16, 64, 128), F32),
            pltpu.VMEM((4, 16, 128), F32),
            pltpu.VMEM((14, 16, 128), F32),
            pltpu.SemaphoreType.DMA((52,)),
            pltpu.SemaphoreType.DMA((52,)),
        ],
        compiler_params=pltpu.CompilerParams(
            collective_id=1, has_side_effects=True, vmem_limit_bytes=VMEM_LIMIT
        ),
        name="reduce",
    )(grads, bias_grad, normed)


def transposed_product(left, right):
    return lax.dot_general(left, right, (((0,), (0,)), ((), ())), preferred_element_type=F32)


WINDOWS = ((0, 0, 5), (128, 5, 3), (384, 8, 5), (512, 13, 3))


def head_mask(start, head):
    lanes = lax.broadcasted_iota(jnp.int32, (64, 256), 1) + start
    return (lanes >= head * 48) & (lanes < head * 48 + 48)


def attention_kernel(
    own_ref, acts_ref, cot_ref, w_ref, bias_ref, valid_ref,
    attended_ref, grads_ref, bias_grad_ref,
    query, key, value, grad, attention, query_grad, key_grad, value_grad, bias_total,
    scores, pulled, weights, probs_low, score_grad,
):
    scaling = 1.0 / math.sqrt(48)
    own = own_ref[...]
    cot = cot_ref[...]
    query[...] = jnp.dot(own, w_ref[0], preferred_element_type=F32).astype(BF16)
    grad[...] = lax.dot_general(
        cot, w_ref[3], (((1,), (1,)), ((), ())), preferred_element_type=F32
    ).astype(BF16)

    def project_rows(block, _):
        rows = pl.ds(pl.multiple_of(block * 256, 256), 256)
        part = acts_ref[rows, :]
        key[rows, :] = jnp.dot(part, w_ref[1], preferred_element_type=F32).astype(BF16)
        value[rows, :] = jnp.dot(part, w_ref[2], preferred_element_type=F32).astype(BF16)
        return 0

    lax.fori_loop(0, 4, project_rows, 0)
    bias_total[...] = jnp.zeros_like(bias_total)
    attention[...] = jnp.zeros_like(attention)
    query_grad[...] = jnp.zeros_like(query_grad)
    key_grad[...] = jnp.zeros_like(key_grad)
    value_grad[...] = jnp.zeros_like(value_grad)
    keep = valid_ref[...] == 1

    def one_copy(s, _):
        q_rows = pl.ds(pl.multiple_of(s * 64, 64), 64)
        k_rows = pl.ds(pl.multiple_of(s * 512, 512), 512)
        for start, first, count in WINDOWS:
            lanes = slice(start, start + 256)
            stacked = slice(0, count * 64)
            k_win = key[k_rows, lanes]
            v_win = value[k_rows, lanes]
            q_win = query[q_rows, lanes]
            g_win = grad[q_rows, lanes]
            masks = [head_mask(start, first + n) for n in range(count)]
            zero = jnp.zeros_like(q_win)
            q_stack = jnp.concatenate([jnp.where(m, q_win, zero) for m in masks], axis=0)
            g_stack = jnp.concatenate([jnp.where(m, g_win, zero) for m in masks], axis=0)
            scores[stacked, :] = lax.dot_general(
                q_stack, k_win, (((1,), (1,)), ((), ())), preferred_element_type=F32
            )
            pulled[stacked, :] = lax.dot_general(
                g_stack, v_win, (((1,), (1,)), ((), ())), preferred_element_type=F32
            )
            inverses = []
            for n in range(count):
                rows = slice(n * 64, n * 64 + 64)
                block = scores[rows, :] * scaling + bias_ref[first + n]
                block = jnp.where(keep, block, MASKED)
                shifted = jnp.exp(block - jnp.max(block, axis=1, keepdims=True))
                inverses.append(1.0 / jnp.sum(shifted, axis=1, keepdims=True))
                scores[rows, :] = shifted
                weights[rows, :] = shifted.astype(BF16)
            merged = jnp.dot(weights[stacked, :], v_win, preferred_element_type=F32)
            attended_win = jnp.zeros((64, 256), F32)
            for n in range(count):
                attended_win = jnp.where(
                    masks[n], merged[n * 64 : n * 64 + 64] * inverses[n], attended_win
                )
            attention[q_rows, lanes] += attended_win
            product = g_win.astype(F32) * attended_win.astype(BF16).astype(F32)
            for n in range(count):
                rows = slice(n * 64, n * 64 + 64)
                delta = jnp.sum(jnp.where(masks[n], product, 0.0), axis=1, keepdims=True)
                probs = scores[rows, :] * inverses[n]
                probs_low[rows, :] = probs.astype(BF16)
                change = (probs * (pulled[rows, :] - delta)).astype(BF16)
                score_grad[rows, :] = change
                bias_total[first + n] += change.astype(F32)
            back = jnp.dot(score_grad[stacked, :], k_win, preferred_element_type=F32)
            back_win = jnp.zeros((64, 256), F32)
            for n in range(count):
                back_win = jnp.where(masks[n], back[n * 64 : n * 64 + 64], back_win)
            query_grad[q_rows, lanes] += back_win
            key_grad[k_rows, lanes] += lax.dot_general(
                score_grad[stacked, :], q_stack, (((0,), (0,)), ((), ())),
                preferred_element_type=F32,
            )
            value_grad[k_rows, lanes] += lax.dot_general(
                probs_low[stacked, :], g_stack, (((0,), (0,)), ((), ())),
                preferred_element_type=F32,
            )
        return 0

    lax.fori_loop(0, 2, one_copy, 0)
    merged_heads = attention[...].astype(BF16)
    attended_ref[...] = jnp.dot(
        merged_heads, w_ref[3], preferred_element_type=F32
    ).astype(BF16)
    q_low = (query_grad[...] * scaling).astype(BF16)
    key[...] = (key_grad[...] * scaling).astype(BF16)
    value[...] = value_grad[...].astype(BF16)
    for block in range(3):
        lanes = slice(block * 256, block * 256 + 256)
        grads_ref[0, lanes, :] = transposed_product(own[:, lanes], q_low).astype(BF16)
        grads_ref[3, lanes, :] = transposed_product(merged_heads[:, lanes], cot).astype(BF16)
        part = acts_ref[:, lanes]
        grads_ref[1, lanes, :] = transposed_product(part, key[...]).astype(BF16)
        grads_ref[2, lanes, :] = transposed_product(part, value[...]).astype(BF16)
    for column in range(4):
        bias_grad_ref[column] = bias_total[:, :, column * 128 : column * 128 + 128].astype(BF16)


def attend(own, acts, cot, weights, bias, valid):
    vmem = pl.BlockSpec(memory_space=pltpu.VMEM)
    return pl.pallas_call(
        attention_kernel,
        out_shape=(
            jax.ShapeDtypeStruct((128, 768), BF16),
            jax.ShapeDtypeStruct((4, 768, 768), BF16),
            jax.ShapeDtypeStruct((4, 16, 64, 128), BF16),
        ),
        in_specs=[vmem] * 6,
        out_specs=[vmem] * 3,
        scratch_shapes=[
            pltpu.VMEM((128, 768), BF16),
            pltpu.VMEM((1024, 768), BF16),
            pltpu.VMEM((1024, 768), BF16),
            pltpu.VMEM((128, 768), BF16),
            pltpu.VMEM((128, 768), F32),
            pltpu.VMEM((128, 768), F32),
            pltpu.VMEM((1024, 768), F32),
            pltpu.VMEM((1024, 768), F32),
            pltpu.VMEM((16, 64, 512), F32),
            pltpu.VMEM((320, 512), F32),
            pltpu.VMEM((320, 512), F32),
            pltpu.VMEM((320, 512), BF16),
            pltpu.VMEM((320, 512), BF16),
            pltpu.VMEM((320, 512), BF16),
        ],
        compiler_params=pltpu.CompilerParams(vmem_limit_bytes=VMEM_LIMIT),
        name="attend",
    )(own, acts, cot, weights, bias, valid)


def per_device(
    single, pair_features, key_valid, pair_gain, w_query, w_key, w_value, w_out, pair_bias_weight,
    out_cotangent,
):
    own_acts = single[0]
    copies, own_count, features = own_acts.shape
    w_all, acts_all, bias, normed = gather(
        jnp.stack((w_query, w_key, w_value, w_out)),
        own_acts,
        pair_features[0],
        pair_gain[None],
        pair_bias_weight.T,
    )
    attended, grads, bias_grad = attend(
        own_acts.reshape(copies * own_count, features),
        acts_all.reshape(copies * 512, features),
        out_cotangent[0].reshape(copies * own_count, features),
        w_all.reshape(4, features, features),
        bias,
        key_valid,
    )
    grads = grads.reshape(4, 4, 2, 4, 24, features)
    results, grad_bias = reduce_all(grads, bias_grad, normed)
    return (
        attended.reshape(1, copies, own_count, features),
        results[0], results[1], results[2], results[3], grad_bias.T,
    )


def solution(mesh):
    weight = P(("row", "col"), None)
    tokens = P("dp", "col", "row", None)
    return jax.shard_map(
        per_device,
        mesh=mesh,
        in_specs=(
            tokens, P("dp", "row", "col", None), P("dp", None), P(), weight, weight, weight, weight,
            P(), tokens,
        ),
        out_specs=(tokens, weight, weight, weight, weight, P()),
        check_vma=False,
    )
```

time: 207 us -> 130 us (0.63)
  local copies, waits for them, and re-layouts: 35.7 us -> 3 us
  matrix products: 30.3 us -> 0 us
  other arithmetic: 12.4 us -> 1.5 us
  Pallas kernels: 127 us -> 124 us
    dot_general x16 -> x0, matrix products: 30.3 us -> none  [the longest x4 10 us: project(): return jnp.dot(flat, matrix, preferred_element_type=F32).astype(BF16)]
    pallas_call x0 -> x1, Pallas kernels: none -> 21.6 us  [attend(): pl.pallas_call(attention_kernel, out_shape=(jax.ShapeDtypeStruct((128, 76...]
    pallas_call x1, Pallas kernels: 68.4 us -> 51.1 us  [reduce_all(): pl.pallas_call(reduce_kernel, out_shape=(jax.ShapeDtypeStruct((4, 24, 768...]
    reshape x7 -> x0, local copies, waits for them, and re-layouts: 12.1 us -> none  [the longest x1 4.01 us: per_device(): value_heads = value_proj.reshape(copies, token_count, head_count, head_size)]
    convert_element_type x7 -> x0, local copies, waits for them, and re-layouts: 9.8 us -> none  [the longest x2 3.37 us: project(): return jnp.dot(flat, matrix, preferred_element_type=F32).astype(BF16)]
    pallas_call x1, Pallas kernels: 58.9 us -> 51.3 us  [gather(): pl.pallas_call(gather_kernel, out_shape=(jax.ShapeDtypeStruct((4, 4, 2, 4...]
    reduce_sum x3 -> x0, other arithmetic: 6.04 us -> none  [the longest x1 2.39 us: normalize_pair(): variance = jnp.mean(centered * centered, axis=-1, keepdims=True)]
    unnamed x53 -> x1, local copies, waits for them, and re-layouts: 6.95 us -> 1.29 us
where the time goes in v2:
time: 130 us; the launch traced here: 129 us
  Pallas kernels  124 us (95%)
  local copies, waits for them, and re-layouts  3 us (2%)
  other arithmetic  1.5 us (1%)
    pallas_call x1, Pallas kernels, gather(): pl.pallas_call(gather_kernel, out_shape=(jax.ShapeDtypeStruct((4, 4, 2, 4...  51.3 us
    pallas_call x1, Pallas kernels, reduce_all(): pl.pallas_call(reduce_kernel, out_shape=(jax.ShapeDtypeStruct((4, 24, 768...  51.1 us
    pallas_call x1, Pallas kernels, attend(): pl.pallas_call(attention_kernel, out_shape=(jax.ShapeDtypeStruct((128, 76...  21.6 us

profile of v2, /device:TPU:2, one launch (start us, length us, event | category | flops | bytes accessed | tf_op | source)
XLA Modules:
  0.0 129.2 jit_solution(3180317788108489870)
XLA Ops:
  0.6 1.5 %pad_maximum_fusion.w_ref = bf16[4,24,768]{2,1,0:T(8,128)(2,1)} fusion(bf16[1,24,768]{2,1,0:T(8,128)(2,1)} %bitcast.30, bf16[1,24,768]{2,1,0:T(8,128)(2,1)} %bitcast.31, bf16[1,24,768]{2,1,0:T(8,128)(2,1)} %bitcast.32, bf16[1,24,768]{2,1,0:T(8,128)(2,1)} %bitcast.33), kind=kLoop, calls=%fused_computation | loop fusion | flops 221184 | bytes 294912 | tf_op jit(solution)/shard_map/stack | solution.py:631
  2.1 51.3 %gather.1 = (bf16[4,4,2,4,24,768]{5,4,3,2,1,0:T(8,128)(2,1)}, bf16[2,8,64,768]{3,2,1,0:T(8,128)(2,1)}, f32[16,64,512]{2,1,0:T(8,128)}, bf16[64,128,128]{2,1,0:T(8,128)(2,1)}) custom-call(bf16[4,24,768]{2,1,0:T(8,128)(2,1)} %pad_maximum_fusion.w_ref, bf16[2,64,768]{2,1,0:T(8,128)(2,1)} %bitcast.27, bf16[64,128,128]{2,1,0:T(8,128)(2,1)} %bitcast.25, ...), custom_call_target="tpu_custom_call" | custom-call | tf_op jit(solution)/shard_map/gather/pallas_call | solution.py:195
  53.4 21.6 %attend.1 = (bf16[128,768]{1,0:T(8,128)(2,1)}, bf16[4,768,768]{2,1,0:T(8,128)(2,1)}, bf16[4,16,64,128]{3,2,1,0:T(8,128)(2,1)}) custom-call(bf16[128,768]{1,0:T(8,128)(2,1)} %bitcast.28, bf16[1024,768]{1,0:T(8,128)(2,1)} %bitcast.26, bf16[128,768]{1,0:T(8,128)(2,1)} %bitcast.29, bf16[4,768,768]{2,1,0:T(8,128)(2,1)} %bitcast.23, ...), custom_call_target="tpu_custom_call" | custom-call | tf_op jit(solution)/shard_map/attend/pallas_call | solution.py:594
  75.1 51.1 %reduce.1 = (f32[4,24,768]{2,1,0:T(8,128)}, f32[16,128]{1,0:T(8,128)}) custom-call(bf16[4,4,2,4,24,768]{5,4,3,2,1,0:T(8,128)(2,1)} %bitcast.24, bf16[4,16,64,128]{3,2,1,0:T(8,128)(2,1)} %get-tuple-element.20.bias_grad_ref, bf16[64,128,128]{2,1,0:T(8,128)(2,1)} %get-tuple-element.21.normed_ref), custom_call_target="tpu_custom_call" | custom-call | tf_op jit(solution)/shard_map/reduce/pallas_call | solution.py:434
  126.2 1.7 %slice_bitcast_fusion = (f32[24,768]{1,0:T(8,128)}, f32[24,768]{1,0:T(8,128)}, f32[24,768]{1,0:T(8,128)}, f32[24,768]{1,0:T(8,128)}) fusion(f32[4,24,768]{2,1,0:T(8,128)} %get-tuple-element.22), kind=kLoop, calls=%fused_computation.1 | loop fusion | bytes 589824 | tf_op jit(solution)/shard_map/squeeze | solution.py:649
  127.9 1.3 %copy.17 = f32[128,16]{0,1:T(8,128)} copy(f32[128,16]{0,1:T(8,128)} %bitcast.34) | data formatting | bytes 16384

commit v3 on v2

--- a/solution.py
+++ b/solution.py
@@ -55,7 +55,7 @@
 
 
 def gather_kernel(
-    w_ref, acts_ref, pair_ref, gain_ref, pair_weight_ref,
+    wq_ref, wk_ref, wv_ref, wo_ref, acts_ref, pair_ref, gain_ref, pair_weight_ref,
     w_full, acts_full, bias_full, normed_ref,
     tile_bias, local_sem, send_sem, recv_sem,
 ):
@@ -99,10 +99,28 @@
     out = Sender(send_sem, recv_sem)
     send = out.send
     first, second = slice(0, 2), slice(2, 4)
-    own_w = pltpu.make_async_copy(w_ref.at[y], w_full.at[y, z_hi, core, x], local_sem.at[0])
+    for plane, w_ref in enumerate((wq_ref, wk_ref, wv_ref, wo_ref)):
+
+        @pl.when(y == plane)
+        def _(plane=plane, w_ref=w_ref):
+            target = w_full.at[plane, z_hi, core, x]
+            pltpu.make_async_copy(w_ref, target, local_sem.at[0]).start()
+            for d, peer in enumerate(z_peers):
+                pltpu.make_async_remote_copy(
+                    src_ref=w_ref, dst_ref=target, send_sem=send_sem.at[d],
+                    recv_sem=recv_sem.at[d], device_id=peer, device_id_type=MESH,
+                ).start()
+
+    own_w = pltpu.make_async_copy(wq_ref, w_full.at[y, z_hi, core, x], local_sem.at[0])
     own_acts = pltpu.make_async_copy(acts_ref, acts_full.at[:, row], local_sem.at[1])
-    own_w.start()
-    z_copies = [send(w_ref.at[y], w_full.at[y, z_hi, core, x], peer) for peer in z_peers]
+    z_copies = [
+        pltpu.make_async_remote_copy(
+            src_ref=wq_ref, dst_ref=w_full.at[y, z_hi, core, x], send_sem=send_sem.at[d],
+            recv_sem=recv_sem.at[d], device_id=peer, device_id_type=MESH,
+        )
+        for d, peer in enumerate(z_peers)
+    ]
+    out.started.extend(z_copies)
     own_acts.start()
     acts_up = send(acts_ref, rows(z_hi), z_next)
     acts_down = send(acts_ref, rows(z_hi), z_back)
@@ -113,6 +131,29 @@
         own = line(y, owner)
         core_copies.append(send(own, own, partner))
         return send(own, own, y_next), send(own, own, y_back)
+
+    def tile_rows(chunk):
+        return slice(chunk * 16, chunk * 16 + 16)
+
+    def bias_block(owner, chunk, heads=slice(0, 16)):
+        return bias_full.at[heads, tile_rows(chunk), columns(owner)]
+
+    bias_near, bias_far = [], []
+
+    def send_bias(chunk):
+        source = tile_bias.at[:, tile_rows(chunk), :]
+        bias_near.append(
+            (send(source, bias_block(x, chunk), x_next), send(source, bias_block(x, chunk), x_back))
+        )
+
+    def relay_bias(chunk):
+        up, down = bias_near[chunk]
+        up.wait_recv()
+        part = bias_block(x + 3, chunk, slice(0, 8))
+        bias_far.append(send(part, part, x_next))
+        down.wait_recv()
+        part = bias_block(x + 1, chunk, slice(8, 16))
+        bias_far.append(send(part, part, x_back))
 
     own_w.wait()
     for copy in z_copies:
@@ -121,7 +162,9 @@
     x_up = send(own, own, x_next)
     x_down = send(own, own, x_back)
     planes = [swap_planes(x)]
+    send_bias(0)
     normalize_rows(1)
+    send_bias(1)
     x_up.wait_recv()
     part = line(y, x + 3, first)
     x_far_up = send(part, part, x_next)
@@ -130,6 +173,8 @@
     x_far_down = send(part, part, x_back)
     planes.append(swap_planes(x + 3))
     planes.append(swap_planes(x + 1))
+    normalize_rows(2)
+    send_bias(2)
     acts_up.wait_recv()
     part = acts_full.at[0, ((z_hi + 3) % 4) * 2 + core]
     acts_far_up = send(part, part, z_next)
@@ -138,6 +183,7 @@
     acts_far_down = send(part, part, z_back)
     core_copies.append(send(rows(z_hi + 3), rows(z_hi + 3), partner))
     core_copies.append(send(rows(z_hi + 1), rows(z_hi + 1), partner))
+    relay_bias(0)
     x_far_up.wait_recv()
     x_far_down.wait_recv()
     planes.append(swap_planes(x + 2))
@@ -158,14 +204,15 @@
             core_copies.append(send(whole, whole, partner))
 
     relay_planes(0)
-    normalize_rows(2)
-    relay_planes(1)
     normalize_rows(3)
+    send_bias(3)
     own_bias = pltpu.make_async_copy(tile_bias, bias_full.at[:, :, columns(x)], local_sem.at[2])
     own_bias.start()
-    bias_up = send(tile_bias, bias_full.at[:, :, columns(x)], x_next)
-    bias_down = send(tile_bias, bias_full.at[:, :, columns(x)], x_back)
+    relay_bias(1)
+    relay_planes(1)
+    relay_bias(2)
     relay_planes(2)
+    relay_bias(3)
     relay_planes(3)
     acts_far_up.wait_recv()
     acts_far_down.wait_recv()
@@ -175,21 +222,14 @@
             copy.wait_recv()
         whole = line(y + 2, owners[n])
         core_copies.append(send(whole, whole, partner))
-        if n == 1:
-            bias_up.wait_recv()
-            part = bias_full.at[slice(0, 8), :, columns(x + 3)]
-            bias_far_up = send(part, part, x_next)
-            bias_down.wait_recv()
-            part = bias_full.at[slice(8, 16), :, columns(x + 1)]
-            bias_far_down = send(part, part, x_back)
-    for copy in core_copies + [bias_far_up, bias_far_down]:
+    for copy in core_copies + bias_far:
         copy.wait_recv()
     own_acts.wait()
     own_bias.wait()
     out.finish()
 
 
-def gather(weights, acts, pair_tile, pair_gain, pair_weight):
+def gather(w_query, w_key, w_value, w_out, acts, pair_tile, pair_gain, pair_weight):
     any_space = pl.BlockSpec(memory_space=pl.ANY)
     vmem = pl.BlockSpec(memory_space=pltpu.VMEM)
     return pl.pallas_call(
@@ -200,19 +240,19 @@
             jax.ShapeDtypeStruct((16, 64, 512), F32),
             jax.ShapeDtypeStruct((64, 128, 128), BF16),
         ),
-        in_specs=[any_space, any_space, vmem, vmem, vmem],
+        in_specs=[any_space] * 5 + [vmem] * 3,
         out_specs=[any_space, any_space, any_space, vmem],
         scratch_shapes=[
             pltpu.VMEM((16, 64, 128), F32),
             pltpu.SemaphoreType.DMA((3,)),
-            pltpu.SemaphoreType.DMA((56,)),
-            pltpu.SemaphoreType.DMA((56,)),
+            pltpu.SemaphoreType.DMA((63,)),
+            pltpu.SemaphoreType.DMA((63,)),
         ],
         compiler_params=pltpu.CompilerParams(
             collective_id=0, has_side_effects=True, vmem_limit_bytes=VMEM_LIMIT
         ),
         name="gather",
-    )(weights, acts, pair_tile, pair_gain, pair_weight)
+    )(w_query, w_key, w_value, w_out, acts, pair_tile, pair_gain, pair_weight)
 
 
 def reduce_kernel(
@@ -485,7 +525,7 @@
     own_ref, acts_ref, cot_ref, w_ref, bias_ref, valid_ref,
     attended_ref, grads_ref, bias_grad_ref,
     query, key, value, grad, attention, query_grad, key_grad, value_grad, bias_total,
-    scores, pulled, weights, probs_low, score_grad,
+    scores, pulled, weights, probs_low, score_grad, joint,
 ):
     scaling = 1.0 / math.sqrt(48)
     own = own_ref[...]
@@ -576,15 +616,16 @@
         merged_heads, w_ref[3], preferred_element_type=F32
     ).astype(BF16)
     q_low = (query_grad[...] * scaling).astype(BF16)
-    key[...] = (key_grad[...] * scaling).astype(BF16)
-    value[...] = value_grad[...].astype(BF16)
+    joint[:, 0:768] = (key_grad[...] * scaling).astype(BF16)
+    joint[:, 768:1536] = value_grad[...].astype(BF16)
     for block in range(3):
         lanes = slice(block * 256, block * 256 + 256)
         grads_ref[0, lanes, :] = transposed_product(own[:, lanes], q_low).astype(BF16)
         grads_ref[3, lanes, :] = transposed_product(merged_heads[:, lanes], cot).astype(BF16)
         part = acts_ref[:, lanes]
-        grads_ref[1, lanes, :] = transposed_product(part, key[...]).astype(BF16)
-        grads_ref[2, lanes, :] = transposed_product(part, value[...]).astype(BF16)
+        both = transposed_product(part, joint[...]).astype(BF16)
+        grads_ref[1, lanes, :] = both[:, 0:768]
+        grads_ref[2, lanes, :] = both[:, 768:1536]
     for column in range(4):
         bias_grad_ref[column] = bias_total[:, :, column * 128 : column * 128 + 128].astype(BF16)
 
@@ -615,6 +656,7 @@
             pltpu.VMEM((320, 512), BF16),
             pltpu.VMEM((320, 512), BF16),
             pltpu.VMEM((320, 512), BF16),
+            pltpu.VMEM((1024, 1536), BF16),
         ],
         compiler_params=pltpu.CompilerParams(vmem_limit_bytes=VMEM_LIMIT),
         name="attend",
@@ -628,8 +670,7 @@
     own_acts = single[0]
     copies, own_count, features = own_acts.shape
     w_all, acts_all, bias, normed = gather(
-        jnp.stack((w_query, w_key, w_value, w_out)),
-        own_acts,
+        w_query, w_key, w_value, w_out, own_acts,
         pair_features[0],
         pair_gain[None],
         pair_bias_weight.T,

time: 130 us -> 123 us (0.946)
  Pallas kernels: 124 us -> 118 us
  other arithmetic: 1.5 us -> 0 us
    pallas_call x1, Pallas kernels: 51.3 us -> 43.9 us  [gather(): pl.pallas_call(gather_kernel, out_shape=(jax.ShapeDtypeStruct((4, 4, 2, 4...]
    pallas_call x1, Pallas kernels: 51.1 us -> 52.8 us  [reduce_all(): pl.pallas_call(reduce_kernel, out_shape=(jax.ShapeDtypeStruct((4, 24, 768...]
    another operation x1 -> x0, other arithmetic: 1.5 us -> none  [per_device(): jnp.stack((w_query, w_key, w_value, w_out))]
where the time goes in v3:
time: 123 us; the launch traced here: 122 us
  Pallas kernels  118 us (96%)
  local copies, waits for them, and re-layouts  3 us (2%)
    pallas_call x1, Pallas kernels, reduce_all(): pl.pallas_call(reduce_kernel, out_shape=(jax.ShapeDtypeStruct((4, 24, 768...  52.8 us
    pallas_call x1, Pallas kernels, gather(): pl.pallas_call(gather_kernel, out_shape=(jax.ShapeDtypeStruct((4, 4, 2, 4...  43.9 us
    pallas_call x1, Pallas kernels, attend(): pl.pallas_call(attention_kernel, out_shape=(jax.ShapeDtypeStruct((128, 76...  21.6 us

profile of v3, /device:TPU:2, one launch (start us, length us, event | category | flops | bytes accessed | tf_op | source)
XLA Modules:
  0.0 121.9 jit_solution(6302320112760237463)
XLA Ops:
  0.6 43.9 %gather.1 = (bf16[4,4,2,4,24,768]{5,4,3,2,1,0:T(8,128)(2,1)}, bf16[2,8,64,768]{3,2,1,0:T(8,128)(2,1)}, f32[16,64,512]{2,1,0:T(8,128)}, bf16[64,128,128]{2,1,0:T(8,128)(2,1)}) custom-call(bf16[24,768]{1,0:T(8,128)(2,1)} %wq_ref.1, bf16[24,768]{1,0:T(8,128)(2,1)} %wk_ref.1, bf16[24,768]{1,0:T(8,128)(2,1)} %wv_ref.1, bf16[24,768]{1,0:T(8,128)(2,1)} %wo_ref.1, ...), custom_call_target="tpu_custom_call" | custom-call | tf_op jit(solution)/shard_map/gather/pallas_call | solution.py:235
  44.6 21.6 %attend.1 = (bf16[128,768]{1,0:T(8,128)(2,1)}, bf16[4,768,768]{2,1,0:T(8,128)(2,1)}, bf16[4,16,64,128]{3,2,1,0:T(8,128)(2,1)}) custom-call(bf16[128,768]{1,0:T(8,128)(2,1)} %bitcast.24, bf16[1024,768]{1,0:T(8,128)(2,1)} %bitcast.22, bf16[128,768]{1,0:T(8,128)(2,1)} %bitcast.25, bf16[4,768,768]{2,1,0:T(8,128)(2,1)} %bitcast.19, ...), custom_call_target="tpu_custom_call" | custom-call | tf_op jit(solution)/shard_map/attend/pallas_call | solution.py:635
  66.2 52.8 %reduce.1 = (f32[4,24,768]{2,1,0:T(8,128)}, f32[16,128]{1,0:T(8,128)}) custom-call(bf16[4,4,2,4,24,768]{5,4,3,2,1,0:T(8,128)(2,1)} %bitcast.20, bf16[4,16,64,128]{3,2,1,0:T(8,128)(2,1)} %get-tuple-element.20.bias_grad_ref, bf16[64,128,128]{2,1,0:T(8,128)(2,1)} %get-tuple-element.21.normed_ref), custom_call_target="tpu_custom_call" | custom-call | tf_op jit(solution)/shard_map/reduce/pallas_call | solution.py:474
  118.9 1.7 %slice_bitcast_fusion = (f32[24,768]{1,0:T(8,128)}, f32[24,768]{1,0:T(8,128)}, f32[24,768]{1,0:T(8,128)}, f32[24,768]{1,0:T(8,128)}) fusion(f32[4,24,768]{2,1,0:T(8,128)} %get-tuple-element.22), kind=kLoop, calls=%fused_computation | loop fusion | bytes 589824 | tf_op jit(solution)/shard_map/squeeze | solution.py:690
  120.6 1.3 %copy.17 = f32[128,16]{0,1:T(8,128)} copy(f32[128,16]{0,1:T(8,128)} %bitcast.26) | data formatting | bytes 16384

commit v4 on v3

v4 whole, which is shorter than its diff:
```python
import math

import jax
import jax.numpy as jnp
from jax import lax
from jax.experimental import pallas as pl
from jax.experimental.pallas import tpu as pltpu
from jax.sharding import PartitionSpec as P

NORM_EPSILON = 1e-05
MASKED = -1000000000.0
MESH = pl.DeviceIdType.MESH
F32 = jnp.float32
BF16 = jnp.bfloat16
VMEM_LIMIT = 56 * 1024 * 1024


def place():
    dp, row, col = lax.axis_index("dp"), lax.axis_index("row"), lax.axis_index("col")
    return dp // 2, dp % 2, row // 2, row % 2, col


def device(y, z_lo, z_hi, core, x):
    return (y * 2 + z_lo, z_hi * 2 + core, x)


def greet(peers):
    barrier = pltpu.get_barrier_semaphore()
    for peer in peers:
        pl.semaphore_signal(barrier, inc=1, device_id=peer, device_id_type=MESH)


def await_greetings(peers):
    pl.semaphore_wait(pltpu.get_barrier_semaphore(), len(peers))


class Sender:
    def __init__(self, send_sem, recv_sem):
        self.send_sem, self.recv_sem, self.started = send_sem, recv_sem, []

    def send(self, src, dst, peer):
        key = len(self.started)
        copy = pltpu.make_async_remote_copy(
            src_ref=src,
            dst_ref=dst,
            send_sem=self.send_sem.at[key],
            recv_sem=self.recv_sem.at[key],
            device_id=peer,
            device_id_type=MESH,
        )
        copy.start()
        self.started.append(copy)
        return copy

    def finish(self):
        for copy in self.started:
            copy.wait_send()


def gather_kernel(
    wq_ref, wk_ref, wv_ref, wo_ref, acts_ref, pair_ref, gain_ref, pair_weight_ref,
    w_full, acts_full, bias_full, normed_ref,
    tile_bias, pair, normed_rows, local_sem, send_sem, recv_sem,
):
    y, z_lo, z_hi, core, x = place()
    row = z_hi * 2 + core
    y_next, y_back = [device((y + d) % 4, z_lo, z_hi, core, x) for d in (1, 3)]
    x_next, x_back = [device(y, z_lo, z_hi, core, (x + d) % 4) for d in (1, 3)]
    z_peers = [device(y, z_lo, (z_hi + d) % 4, core, x) for d in (1, 2, 3)]
    z_next, z_back = z_peers[0], z_peers[2]
    partner = device(y, z_lo, z_hi, 1 - core, x)
    peers = [y_next, y_back, x_next, x_back, partner] + z_peers
    greet(peers)

    def block_rows(block):
        return slice(block * 16, block * 16 + 16)

    loads = [
        pltpu.make_async_copy(
            pair_ref.at[block_rows(b)], pair.at[block_rows(b)], local_sem.at[3 + b]
        )
        for b in range(4)
    ]
    for load in loads:
        load.start()
    stores = []
    await_greetings(peers)

    def normalize_rows(block):
        loads[block].wait()

        def one_row(k, _):
            i = block * 16 + k
            values = pair[i].astype(F32)
            center = jnp.mean(values, axis=-1, keepdims=True)
            centered = values - center
            variance = jnp.mean(centered * centered, axis=-1, keepdims=True)
            normed = (
                centered * lax.rsqrt(variance + NORM_EPSILON) * gain_ref[...]
            ).astype(BF16)
            normed_rows[i] = normed
            tile_bias[block, :, k, :] = lax.dot_general(
                pair_weight_ref[...], normed, (((1,), (1,)), ((), ())),
                preferred_element_type=F32,
            )
            return 0

        lax.fori_loop(0, 16, one_row, 0, unroll=4)
        store = pltpu.make_async_copy(
            normed_rows.at[block_rows(block)], normed_ref.at[block_rows(block)],
            local_sem.at[7 + block],
        )
        store.start()
        stores.append(store)

    def line(plane, owner, part=slice(0, 4)):
        return w_full.at[plane % 4, part, core, owner % 4]

    def rows(z_owner):
        return acts_full.at[:, (z_owner % 4) * 2 + core]

    out = Sender(send_sem, recv_sem)
    send = out.send
    first, second = slice(0, 2), slice(2, 4)
    for plane, w_ref in enumerate((wq_ref, wk_ref, wv_ref, wo_ref)):

        @pl.when(y == plane)
        def _(plane=plane, w_ref=w_ref):
            target = w_full.at[plane, z_hi, core, x]
            pltpu.make_async_copy(w_ref, target, local_sem.at[0]).start()
            for d, peer in enumerate(z_peers):
                pltpu.make_async_remote_copy(
                    src_ref=w_ref, dst_ref=target, send_sem=send_sem.at[d],
                    recv_sem=recv_sem.at[d], device_id=peer, device_id_type=MESH,
                ).start()

    own_w = pltpu.make_async_copy(wq_ref, w_full.at[y, z_hi, core, x], local_sem.at[0])
    own_acts = pltpu.make_async_copy(acts_ref, acts_full.at[:, row], local_sem.at[1])
    z_copies = [
        pltpu.make_async_remote_copy(
            src_ref=wq_ref, dst_ref=w_full.at[y, z_hi, core, x], send_sem=send_sem.at[d],
            recv_sem=recv_sem.at[d], device_id=peer, device_id_type=MESH,
        )
        for d, peer in enumerate(z_peers)
    ]
    out.started.extend(z_copies)
    own_acts.start()
    acts_up = send(acts_ref, rows(z_hi), z_next)
    acts_down = send(acts_ref, rows(z_hi), z_back)
    core_copies = [send(acts_ref, rows(z_hi), partner)]
    normalize_rows(0)

    def swap_planes(owner):
        own = line(y, owner)
        core_copies.append(send(own, own, partner))
        return send(own, own, y_next), send(own, own, y_back)

    def bias_block(owner, chunk, heads=slice(0, 16)):
        return bias_full.at[chunk, owner % 4, heads]

    bias_near, bias_far = [], []

    def send_bias(chunk):
        source = tile_bias.at[chunk]
        bias_near.append(
            (send(source, bias_block(x, chunk), x_next), send(source, bias_block(x, chunk), x_back))
        )

    def relay_bias(chunk):
        up, down = bias_near[chunk]
        up.wait_recv()
        part = bias_block(x + 3, chunk, slice(0, 8))
        bias_far.append(send(part, part, x_next))
        down.wait_recv()
        part = bias_block(x + 1, chunk, slice(8, 16))
        bias_far.append(send(part, part, x_back))

    own_w.wait()
    for copy in z_copies:
        copy.wait_recv()
    own = line(y, x)
    x_up = send(own, own, x_next)
    x_down = send(own, own, x_back)
    planes = [swap_planes(x)]
    send_bias(0)
    normalize_rows(1)
    send_bias(1)
    x_up.wait_recv()
    part = line(y, x + 3, first)
    x_far_up = send(part, part, x_next)
    x_down.wait_recv()
    part = line(y, x + 1, second)
    x_far_down = send(part, part, x_back)
    planes.append(swap_planes(x + 3))
    planes.append(swap_planes(x + 1))
    normalize_rows(2)
    send_bias(2)
    acts_up.wait_recv()
    part = acts_full.at[0, ((z_hi + 3) % 4) * 2 + core]
    acts_far_up = send(part, part, z_next)
    acts_down.wait_recv()
    part = acts_full.at[1, ((z_hi + 1) % 4) * 2 + core]
    acts_far_down = send(part, part, z_back)
    core_copies.append(send(rows(z_hi + 3), rows(z_hi + 3), partner))
    core_copies.append(send(rows(z_hi + 1), rows(z_hi + 1), partner))
    relay_bias(0)
    x_far_up.wait_recv()
    x_far_down.wait_recv()
    planes.append(swap_planes(x + 2))
    owners = (x, x + 3, x + 1, x + 2)
    far = []

    def relay_planes(n):
        up, down = planes[n]
        owner = owners[n]
        up.wait_recv()
        part = line(y + 3, owner, first)
        far_up = send(part, part, y_next)
        down.wait_recv()
        part = line(y + 1, owner, second)
        far.append((far_up, send(part, part, y_back)))
        for plane in (y + 3, y + 1):
            whole = line(plane, owner)
            core_copies.append(send(whole, whole, partner))

    relay_planes(0)
    normalize_rows(3)
    send_bias(3)
    own_bias = pltpu.make_async_copy(tile_bias, bias_full.at[:, x], local_sem.at[2])
    own_bias.start()
    relay_bias(1)
    relay_planes(1)
    relay_bias(2)
    relay_planes(2)
    relay_bias(3)
    relay_planes(3)
    acts_far_up.wait_recv()
    acts_far_down.wait_recv()
    core_copies.append(send(rows(z_hi + 2), rows(z_hi + 2), partner))
    for n in range(4):
        for copy in far[n]:
            copy.wait_recv()
        whole = line(y + 2, owners[n])
        core_copies.append(send(whole, whole, partner))
    for copy in core_copies + bias_far:
        copy.wait_recv()
    own_acts.wait()
    own_bias.wait()
    for store in stores:
        store.wait()
    out.finish()


def gather(w_query, w_key, w_value, w_out, acts, pair_tile, pair_gain, pair_weight):
    any_space = pl.BlockSpec(memory_space=pl.ANY)
    vmem = pl.BlockSpec(memory_space=pltpu.VMEM)
    return pl.pallas_call(
        gather_kernel,
        out_shape=(
            jax.ShapeDtypeStruct((4, 4, 2, 4, 24, 768), BF16),
            jax.ShapeDtypeStruct((2, 8, 64, 768), BF16),
            jax.ShapeDtypeStruct((4, 4, 16, 16, 128), F32),
            jax.ShapeDtypeStruct((64, 128, 128), BF16),
        ),
        in_specs=[any_space] * 6 + [vmem] * 2,
        out_specs=[any_space] * 4,
        scratch_shapes=[
            pltpu.VMEM((4, 16, 16, 128), F32),
            pltpu.VMEM((64, 128, 128), BF16),
            pltpu.VMEM((64, 128, 128), BF16),
            pltpu.SemaphoreType.DMA((11,)),
            pltpu.SemaphoreType.DMA((63,)),
            pltpu.SemaphoreType.DMA((63,)),
        ],
        compiler_params=pltpu.CompilerParams(
            collective_id=0, has_side_effects=True, vmem_limit_bytes=VMEM_LIMIT
        ),
        name="gather",
    )(w_query, w_key, w_value, w_out, acts, pair_tile, pair_gain, pair_weight)


def transposed_product(left, right):
    return lax.dot_general(left, right, (((0,), (0,)), ((), ())), preferred_element_type=F32)


WINDOWS = ((0, 0, 5), (128, 5, 3), (384, 8, 5), (512, 13, 3))


def head_mask(start, head):
    lanes = lax.broadcasted_iota(jnp.int32, (64, 256), 1) + start
    return (lanes >= head * 48) & (lanes < head * 48 + 48)


def attention_kernel(
    own_ref, cot_ref, valid_ref, acts_hbm, w_hbm, bias_hbm, normed_hbm,
    attended_ref, gq_ref, gk_ref, gv_ref, go_ref, bias_out_ref,
    acts_ref, w_ref, bias_ref, normed_ref,
    query, key, value, grad, attention, query_grad, key_grad, value_grad, bias_total,
    scores, pulled, weights, probs_low, score_grad, joint, bias_grad,
    g_ref, from_core, to_far, from_far, to_y, from_y, to_x, from_x, x_halves, to_z, from_z,
    own_sum, last, from_last, results,
    bias_halves, bias_sent, bias_in, bias_sum, partial, partial_in,
    local_sem, send_sem, recv_sem,
):
    y, z_lo, z_hi, core, x = place()
    z = z_hi * 2 + z_lo
    y_peers = [device((y + d) % 4, z_lo, z_hi, core, x) for d in (1, 2, 3)]
    x_peers = [device(y, z_lo, z_hi, core, (x + d) % 4) for d in (1, 2, 3)]
    z_peers = [device(y, (z + d) % 2, ((z + d) % 8) // 2, core, x) for d in range(1, 8)]
    partner = device(y, z_lo, z_hi, 1 - core, x)
    y_next, y_back, x_next, x_back = y_peers[0], y_peers[2], x_peers[0], x_peers[2]
    peers = y_peers + x_peers + z_peers + [partner]
    greet(peers)

    load_acts = pltpu.make_async_copy(acts_hbm, acts_ref, local_sem.at[0])
    load_w = [
        pltpu.make_async_copy(w_hbm.at[n], w_ref.at[n], local_sem.at[1 + n]) for n in range(4)
    ]
    load_bias = pltpu.make_async_copy(bias_hbm, bias_ref, local_sem.at[5])
    load_normed = pltpu.make_async_copy(normed_hbm, normed_ref, local_sem.at[6])
    load_w[3].start()
    load_w[0].start()
    load_acts.start()
    load_w[1].start()
    load_w[2].start()
    load_bias.start()
    load_normed.start()

    scaling = 1.0 / math.sqrt(48)
    own = own_ref[...]
    cot = cot_ref[...]
    bias_total[...] = jnp.zeros_like(bias_total)
    attention[...] = jnp.zeros_like(attention)
    query_grad[...] = jnp.zeros_like(query_grad)
    key_grad[...] = jnp.zeros_like(key_grad)
    value_grad[...] = jnp.zeros_like(value_grad)
    load_w[3].wait()
    grad[...] = lax.dot_general(
        cot, w_ref[3], (((1,), (1,)), ((), ())), preferred_element_type=F32
    ).astype(BF16)
    load_w[0].wait()
    query[...] = jnp.dot(own, w_ref[0], preferred_element_type=F32).astype(BF16)
    load_acts.wait()
    load_w[1].wait()
    load_w[2].wait()

    def project_rows(block, _):
        rows = pl.ds(pl.multiple_of(block * 256, 256), 256)
        part = acts_ref[rows, :]
        key[rows, :] = jnp.dot(part, w_ref[1], preferred_element_type=F32).astype(BF16)
        value[rows, :] = jnp.dot(part, w_ref[2], preferred_element_type=F32).astype(BF16)
        return 0

    lax.fori_loop(0, 4, project_rows, 0)
    load_bias.wait()
    keep = valid_ref[...] == 1

    def head_bias(head):
        return jnp.concatenate(
            [
                jnp.concatenate([bias_ref[r, c, head] for c in range(4)], axis=1)
                for r in range(4)
            ],
            axis=0,
        )

    def one_copy(s, _):
        q_rows = pl.ds(pl.multiple_of(s * 64, 64), 64)
        k_rows = pl.ds(pl.multiple_of(s * 512, 512), 512)
        for start, first, count in WINDOWS:
            lanes = slice(start, start + 256)
            stacked = slice(0, count * 64)
            k_win = key[k_rows, lanes]
            v_win = value[k_rows, lanes]
            q_win = query[q_rows, lanes]
            g_win = grad[q_rows, lanes]
            masks = [head_mask(start, first + n) for n in range(count)]
            zero = jnp.zeros_like(q_win)
            q_stack = jnp.concatenate([jnp.where(m, q_win, zero) for m in masks], axis=0)
            g_stack = jnp.concatenate([jnp.where(m, g_win, zero) for m in masks], axis=0)
            scores[stacked, :] = lax.dot_general(
                q_stack, k_win, (((1,), (1,)), ((), ())), preferred_element_type=F32
            )
            pulled[stacked, :] = lax.dot_general(
                g_stack, v_win, (((1,), (1,)), ((), ())), preferred_element_type=F32
            )
            inverses = []
            for n in range(count):
                rows = slice(n * 64, n * 64 + 64)
                block = scores[rows, :] * scaling + head_bias(first + n)
                block = jnp.where(keep, block, MASKED)
                shifted = jnp.exp(block - jnp.max(block, axis=1, keepdims=True))
                inverses.append(1.0 / jnp.sum(shifted, axis=1, keepdims=True))
                scores[rows, :] = shifted
                weights[rows, :] = shifted.astype(BF16)
            merged = jnp.dot(weights[stacked, :], v_win, preferred_element_type=F32)
            attended_win = jnp.zeros((64, 256), F32)
            for n in range(count):
                attended_win = jnp.where(
                    masks[n], merged[n * 64 : n * 64 + 64] * inverses[n], attended_win
                )
            attention[q_rows, lanes] += attended_win
            product = g_win.astype(F32) * attended_win.astype(BF16).astype(F32)
            for n in range(count):
                rows = slice(n * 64, n * 64 + 64)
                delta = jnp.sum(jnp.where(masks[n], product, 0.0), axis=1, keepdims=True)
                probs = scores[rows, :] * inverses[n]
                probs_low[rows, :] = probs.astype(BF16)
                change = (probs * (pulled[rows, :] - delta)).astype(BF16)
                score_grad[rows, :] = change
                bias_total[first + n] += change.astype(F32)
            back = jnp.dot(score_grad[stacked, :], k_win, preferred_element_type=F32)
            back_win = jnp.zeros((64, 256), F32)
            for n in range(count):
                back_win = jnp.where(masks[n], back[n * 64 : n * 64 + 64], back_win)
            query_grad[q_rows, lanes] += back_win
            key_grad[k_rows, lanes] += lax.dot_general(
                score_grad[stacked, :], q_stack, (((0,), (0,)), ((), ())),
                preferred_element_type=F32,
            )
            value_grad[k_rows, lanes] += lax.dot_general(
                probs_low[stacked, :], g_stack, (((0,), (0,)), ((), ())),
                preferred_element_type=F32,
            )
        return 0

    lax.fori_loop(0, 2, one_copy, 0)
    await_greetings(peers)
    out = Sender(send_sem, recv_sem)
    send = out.send

    for column in range(4):
        bias_grad[column] = bias_total[:, :, column * 128 : column * 128 + 128].astype(BF16)
    far_block = bias_grad.at[(x + 2) % 4]
    bias_far = [
        send(far_block.at[slice(0, 8)], bias_halves.at[0], x_next),
        send(far_block.at[slice(8, 16)], bias_halves.at[1], x_back),
    ]

    merged_heads = attention[...].astype(BF16)
    q_low = (query_grad[...] * scaling).astype(BF16)
    joint[:, 0:768] = (key_grad[...] * scaling).astype(BF16)
    joint[:, 768:1536] = value_grad[...].astype(BF16)
    core_copies = {}

    def store_grads(w, half, product):
        g_ref[w, 2 * half : 2 * half + 2] = product.reshape(2, 2, 4, 24, 768).astype(BF16)
        part = slice(2 * half, 2 * half + 2)
        core_copies[w, half] = send(
            g_ref.at[w, part, 1 - core], from_core.at[w, part], partner
        )

    def own_products(half):
        lanes = slice(half * 384, half * 384 + 384)
        store_grads(3, half, transposed_product(merged_heads[:, lanes], cot))
        store_grads(0, half, transposed_product(own[:, lanes], q_low))

    def all_products(half):
        lanes = slice(half * 384, half * 384 + 384)
        both = transposed_product(acts_ref[:, lanes], joint[...])
        store_grads(1, half, both[:, 0:768])
        store_grads(2, half, both[:, 768:1536])

    def both_cores(f, w, k):
        c = (x + f) % 4
        return g_ref[w, k, core, c].astype(F32) + from_core[w, k, c].astype(F32)

    far, near = {}, {}

    def start_chunk(half, f):
        if f == 2:
            for w in range(4):
                core_copies[w, half].wait_recv()
        for k in (2 * half, 2 * half + 1):
            to_far[f, k] = both_cores(f, (y + 2) % 4, k).astype(BF16)
        far[half, f] = (
            send(to_far.at[f, 2 * half], from_far.at[0, half, f], y_next),
            send(to_far.at[f, 2 * half + 1], from_far.at[1, half, f], y_back),
        )

    def pass_chunk(half, f):
        up, down = (y + 1) % 4, (y + 3) % 4
        one, two = 2 * half, 2 * half + 1
        to_y[0, half, f, 1] = both_cores(f, up, two).astype(BF16)
        to_y[1, half, f, 0] = both_cores(f, down, one).astype(BF16)
        far[half, f][0].wait_recv()
        to_y[0, half, f, 0] = (
            both_cores(f, up, one) + from_far[0, half, f].astype(F32)
        ).astype(BF16)
        up_copy = send(to_y.at[0, half, f], from_y.at[0, half, f], y_next)
        far[half, f][1].wait_recv()
        to_y[1, half, f, 1] = (
            both_cores(f, down, two) + from_far[1, half, f].astype(F32)
        ).astype(BF16)
        near[half, f] = (up_copy, send(to_y.at[1, half, f], from_y.at[1, half, f], y_back))

    own_products(0)
    all_products(0)
    own_products(1)
    start_chunk(0, 2)
    start_chunk(0, 1)
    all_products(1)
    pass_chunk(0, 2)
    start_chunk(0, 3)
    pass_chunk(0, 1)
    start_chunk(0, 0)
    for copy in bias_far:
        copy.wait_recv()

    def add_bias(h, _):
        up, down = (x + 1) % 4, (x + 3) % 4
        bias_sent[0, h] = (
            bias_grad[up, h].astype(F32) + bias_halves[0, h].astype(F32)
        ).astype(BF16)
        bias_sent[0, h + 8] = bias_grad[up, h + 8]
        bias_sent[1, h] = bias_grad[down, h]
        bias_sent[1, h + 8] = (
            bias_grad[down, h + 8].astype(F32) + bias_halves[1, h].astype(F32)
        ).astype(BF16)
        return 0

    lax.fori_loop(0, 8, add_bias, 0)
    bias_near = [
        send(bias_sent.at[0], bias_in.at[0], x_next),
        send(bias_sent.at[1], bias_in.at[1], x_back),
    ]
    pass_chunk(0, 3)
    pass_chunk(0, 0)
    attended_ref[...] = jnp.dot(merged_heads, w_ref[3], preferred_element_type=F32).astype(BF16)
    start_chunk(1, 2)
    start_chunk(1, 1)
    pass_chunk(1, 2)
    start_chunk(1, 3)
    pass_chunk(1, 1)
    start_chunk(1, 0)
    pass_chunk(1, 3)

    for copy in bias_near:
        copy.wait_recv()

    def sum_bias(h, _):
        summed = (
            bias_grad[x, h].astype(F32) + bias_in[0, h].astype(F32) + bias_in[1, h].astype(F32)
        )
        bias_sum[h] = summed.astype(BF16).astype(F32)
        return 0

    lax.fori_loop(0, 16, sum_bias, 0)
    load_normed.wait()

    def tile_rows(block, total):
        for u in range(8):
            i = block * 8 + u
            total = total + jnp.dot(
                bias_sum[:, i, :].astype(BF16), normed_ref[i], preferred_element_type=F32
            )
        return total

    early = lax.fori_loop(0, 4, tile_rows, jnp.zeros((16, 128), F32))
    pass_chunk(1, 0)
    partial[0] = lax.fori_loop(4, 8, tile_rows, early)
    stages = ([partner], y_peers, x_peers, z_peers)
    starts = (0, 1, 4, 7)
    in_flight = {}

    def start_stage(n):
        in_flight[n] = [
            send(partial.at[n], partial_in.at[starts[n] + d], peer)
            for d, peer in enumerate(stages[n])
        ]

    def end_stage(n):
        total = partial[n]
        for d, copy in enumerate(in_flight[n]):
            copy.wait_recv()
            total = total + partial_in[starts[n] + d]
        if n < 3:
            partial[n + 1] = total
            start_stage(n + 1)
        else:
            bias_out_ref[...] = total.T

    def all_planes(half, f, n):
        return (
            both_cores(f, y, 2 * half + n)
            + from_y[0, half, f, n].astype(F32)
            + from_y[1, half, f, n].astype(F32)
        )

    def wait_planes(half, f):
        near[half, f][0].wait_recv()
        near[half, f][1].wait_recv()

    x_far, x_near = {}, {}

    def start_column(half):
        wait_planes(half, 2)
        for n in range(2):
            to_x[2, half, n] = all_planes(half, 2, n).astype(BF16)
        x_far[half] = (
            send(to_x.at[2, half, 0], x_halves.at[0, half], x_next),
            send(to_x.at[2, half, 1], x_halves.at[1, half], x_back),
        )

    def pass_column(half):
        wait_planes(half, 1)
        to_x[0, half, 1] = all_planes(half, 1, 1).astype(BF16)
        x_far[half][0].wait_recv()
        to_x[0, half, 0] = (
            all_planes(half, 1, 0) + x_halves[0, half].astype(F32)
        ).astype(BF16)
        up = send(to_x.at[0, half], from_x.at[0, half], x_next)
        wait_planes(half, 3)
        to_x[1, half, 0] = all_planes(half, 3, 0).astype(BF16)
        x_far[half][1].wait_recv()
        to_x[1, half, 1] = (
            all_planes(half, 3, 1) + x_halves[1, half].astype(F32)
        ).astype(BF16)
        x_near[half] = (up, send(to_x.at[1, half], from_x.at[1, half], x_back))

    def end_column(half):
        wait_planes(half, 0)
        for copy in x_near[half]:
            copy.wait_recv()
        for n in range(2):
            total = (
                all_planes(half, 0, n)
                + from_x[0, half, n].astype(F32)
                + from_x[1, half, n].astype(F32)
            )
            own_sum[2 * half + n] = total
            to_z[2 * half + n] = total.astype(BF16)

    start_stage(0)
    start_column(0)
    end_stage(0)
    pass_column(0)
    end_stage(1)
    start_column(1)
    pass_column(1)
    end_column(0)
    end_stage(2)
    end_column(1)
    z_copies = []
    for d in range(7):
        target = ((z + 1 + d) % 8) // 2
        z_copies.append(send(to_z.at[target], from_z.at[d], z_peers[d]))
    end_stage(3)
    total = own_sum[z_hi]
    for d, copy in enumerate(z_copies):
        copy.wait_recv()
        total = total + from_z[d].astype(F32)
    last[...] = total.astype(BF16)
    last_copies = [send(last, from_last.at[d], y_peers[d]) for d in range(3)]
    results[y] = total.astype(BF16).astype(F32)
    for d, copy in enumerate(last_copies):
        copy.wait_recv()
        results[(y + 3 - d) % 4] = from_last[d].astype(F32)
    for n, ref in enumerate((gq_ref, gk_ref, gv_ref, go_ref)):
        ref[...] = results[n]
    out.finish()


def attend(own, cot, valid, acts, weights, bias, normed):
    vmem = pl.BlockSpec(memory_space=pltpu.VMEM)
    any_space = pl.BlockSpec(memory_space=pl.ANY)
    grads = jax.ShapeDtypeStruct((24, 768), F32)
    return pl.pallas_call(
        attention_kernel,
        out_shape=(
            jax.ShapeDtypeStruct((128, 768), BF16),
            grads, grads, grads, grads,
            jax.ShapeDtypeStruct((128, 16), F32),
        ),
        in_specs=[vmem] * 3 + [any_space] * 4,
        out_specs=[vmem] * 6,
        scratch_shapes=[
            pltpu.VMEM((1024, 768), BF16),
            pltpu.VMEM((4, 768, 768), BF16),
            pltpu.VMEM((4, 4, 16, 16, 128), F32),
            pltpu.VMEM((64, 128, 128), BF16),
            pltpu.VMEM((128, 768), BF16),
            pltpu.VMEM((1024, 768), BF16),
            pltpu.VMEM((1024, 768), BF16),
            pltpu.VMEM((128, 768), BF16),
            pltpu.VMEM((128, 768), F32),
            pltpu.VMEM((128, 768), F32),
            pltpu.VMEM((1024, 768), F32),
            pltpu.VMEM((1024, 768), F32),
            pltpu.VMEM((16, 64, 512), F32),
            pltpu.VMEM((320, 512), F32),
            pltpu.VMEM((320, 512), F32),
            pltpu.VMEM((320, 512), BF16),
            pltpu.VMEM((320, 512), BF16),
            pltpu.VMEM((320, 512), BF16),
            pltpu.VMEM((1024, 1536), BF16),
            pltpu.VMEM((4, 16, 64, 128), BF16),
            pltpu.VMEM((4, 4, 2, 4, 24, 768), BF16),
            pltpu.VMEM((4, 4, 4, 24, 768), BF16),
            pltpu.VMEM((4, 4, 24, 768), BF16),
            pltpu.VMEM((2, 2, 4, 24, 768), BF16),
            pltpu.VMEM((2, 2, 4, 2, 24, 768), BF16),
            pltpu.VMEM((2, 2, 4, 2, 24, 768), BF16),
            pltpu.VMEM((3, 2, 2, 24, 768), BF16),
            pltpu.VMEM((2, 2, 2, 24, 768), BF16),
            pltpu.VMEM((2, 2, 24, 768), BF16),
            pltpu.VMEM((4, 24, 768), BF16),
            pltpu.VMEM((7, 24, 768), BF16),
            pltpu.VMEM((4, 24, 768), F32),
            pltpu.VMEM((24, 768), BF16),
            pltpu.VMEM((3, 24, 768), BF16),
            pltpu.VMEM((4, 24, 768), F32),
            pltpu.VMEM((2, 8, 64, 128), BF16),
            pltpu.VMEM((2, 16, 64, 128), BF16),
            pltpu.VMEM((2, 16, 64, 128), BF16),
            pltpu.VMEM((16, 64, 128), F32),
            pltpu.VMEM((4, 16, 128), F32),
            pltpu.VMEM((14, 16, 128), F32),
            pltpu.SemaphoreType.DMA((7,)),
            pltpu.SemaphoreType.DMA((76,)),
            pltpu.SemaphoreType.DMA((76,)),
        ],
        compiler_params=pltpu.CompilerParams(
            collective_id=1, has_side_effects=True, vmem_limit_bytes=VMEM_LIMIT
        ),
        name="attend",
    )(own, cot, valid, acts, weights, bias, normed)


def per_device(
    single, pair_features, key_valid, pair_gain, w_query, w_key, w_value, w_out, pair_bias_weight,
    out_cotangent,
):
    own_acts = single[0]
    copies, own_count, features = own_acts.shape
    w_all, acts_all, bias, normed = gather(
        w_query, w_key, w_value, w_out, own_acts,
        pair_features[0],
        pair_gain[None],
        pair_bias_weight.T,
    )
    attended, grad_query, grad_key, grad_value, grad_out, grad_bias = attend(
        own_acts.reshape(copies * own_count, features),
        out_cotangent[0].reshape(copies * own_count, features),
        key_valid,
        acts_all.reshape(copies * 512, features),
        w_all.reshape(4, features, features),
        bias,
        normed,
    )
    attended = attended.reshape(1, copies, own_count, features)
    return (attended, grad_query, grad_key, grad_value, grad_out, grad_bias)


def solution(mesh):
    weight = P(("row", "col"), None)
    tokens = P("dp", "col", "row", None)
    return jax.shard_map(
        per_device,
        mesh=mesh,
        in_specs=(
            tokens, P("dp", "row", "col", None), P("dp", None), P(), weight, weight, weight, weight,
            P(), tokens,
        ),
        out_specs=(tokens, weight, weight, weight, weight, P()),
        check_vma=False,
    )
```

time: 123 us -> 123 us (level)
  local copies, waits for them, and re-layouts: 3 us -> 9.21 us
  Pallas kernels: 118 us -> 113 us
    pallas_call x1 -> x0, Pallas kernels: 52.8 us -> none  [reduce_all(): pl.pallas_call(reduce_kernel, out_shape=(jax.ShapeDtypeStruct((4, 24, 768...]
    pallas_call x1, Pallas kernels: 21.6 us -> 70.8 us  [attend(): pl.pallas_call(attention_kernel, out_shape=(jax.ShapeDtypeStruct((128, 76...]
    unnamed x1 -> x6, local copies, waits for them, and re-layouts: 1.29 us -> 9.21 us
    pallas_call x1, Pallas kernels: 43.9 us -> 41.8 us  [gather(): pl.pallas_call(gather_kernel, out_shape=(jax.ShapeDtypeStruct((4, 4, 2, 4...]
    squeeze x1 -> x0, local copies, waits for them, and re-layouts: 1.71 us -> none  [per_device(): results[3]]
where the time goes in v4:
time: 123 us; the launch traced here: 122 us
  Pallas kernels  113 us (92%)
  local copies, waits for them, and re-layouts  9.21 us (7%)
    pallas_call x1, Pallas kernels, attend(): pl.pallas_call(attention_kernel, out_shape=(jax.ShapeDtypeStruct((128, 76...  70.8 us
    pallas_call x1, Pallas kernels, gather(): pl.pallas_call(gather_kernel, out_shape=(jax.ShapeDtypeStruct((4, 4, 2, 4...  41.8 us
    unnamed x6, local copies, waits for them, and re-layouts  9.21 us

profile of v4, /device:TPU:2, one launch (start us, length us, event | category | flops | bytes accessed | tf_op | source)
XLA Modules:
  0.0 122.4 jit_solution(14170049424446066126)
XLA Ops:
  0.6 41.8 %gather.1 = (bf16[4,4,2,4,24,768]{5,4,3,2,1,0:T(8,128)(2,1)}, bf16[2,8,64,768]{3,2,1,0:T(8,128)(2,1)}, f32[4,4,16,16,128]{4,3,2,1,0:T(8,128)}, bf16[64,128,128]{2,1,0:T(8,128)(2,1)}) custom-call(bf16[24,768]{1,0:T(8,128)(2,1)} %wq_ref.1, bf16[24,768]{1,0:T(8,128)(2,1)} %wk_ref.1, bf16[24,768]{1,0:T(8,128)(2,1)} %wv_ref.1, bf16[24,768]{1,0:T(8,128)(2,1)} %wo_ref.1, ...), custom_call_target="tpu_custom_call" | custom-call | tf_op jit(solution)/shard_map/gather/pallas_call | solution.py:257
  42.4 70.8 %attend.1 = (bf16[128,768]{1,0:T(8,128)(2,1)}, f32[24,768]{1,0:T(8,128)}, f32[24,768]{1,0:T(8,128)}, f32[24,768]{1,0:T(8,128)}, f32[24,768]{1,0:T(8,128)}, /*index=5*/f32[128,16]{1,0:T(8,128)}) custom-call(bf16[128,768]{1,0:T(8,128)(2,1)} %bitcast.13, bf16[128,768]{1,0:T(8,128)(2,1)} %bitcast.15, s32[1,512]{1,0:T(1,128)} %valid_ref.1, ...), custom_call_target="tpu_custom_call" | custom-call | tf_op jit(solution)/shard_map/attend/pallas_call | solution.py:668
  113.2 1.5 %copy.16 = f32[128,16]{0,1:T(8,128)} copy(f32[128,16]{1,0:T(8,128)} %get-tuple-element.31) | data formatting | bytes 16384
  114.7 1.6 %copy.22 = bf16[1,2,64,768]{3,2,1,0:T(8,128)(2,1)} copy(bf16[1,2,64,768]{3,2,1,0:T(8,128)(2,1)} %bitcast.14) | data formatting | bytes 393216
  116.3 1.5 %copy.23 = f32[24,768]{1,0:T(8,128)} copy(f32[24,768]{1,0:T(8,128)} %get-tuple-element.39) | data formatting | bytes 147456
  117.8 1.5 %copy.24 = f32[24,768]{1,0:T(8,128)} copy(f32[24,768]{1,0:T(8,128)} %get-tuple-element.40) | data formatting | bytes 147456
  119.3 1.5 %copy.25 = f32[24,768]{1,0:T(8,128)} copy(f32[24,768]{1,0:T(8,128)} %get-tuple-element.41) | data formatting | bytes 147456
  120.9 1.5 %copy.26 = f32[24,768]{1,0:T(8,128)} copy(f32[24,768]{1,0:T(8,128)} %get-tuple-element.42) | data formatting | bytes 147456

commit v5 on v4

--- a/solution.py
+++ b/solution.py
@@ -293,23 +293,23 @@
 
 def attention_kernel(
     own_ref, cot_ref, valid_ref, acts_hbm, w_hbm, bias_hbm, normed_hbm,
-    attended_ref, gq_ref, gk_ref, gv_ref, go_ref, bias_out_ref,
+    attended_ref, results, bias_out_ref,
     acts_ref, w_ref, bias_ref, normed_ref,
     query, key, value, grad, attention, query_grad, key_grad, value_grad, bias_total,
     scores, pulled, weights, probs_low, score_grad, joint, bias_grad,
-    g_ref, from_core, to_far, from_far, to_y, from_y, to_x, from_x, x_halves, to_z, from_z,
-    own_sum, last, from_last, results,
+    g_ref, from_core, to_far, from_far, to_y, from_y, to_x, from_x, x_halves,
+    own_sum, to_pair, from_pair, to_z, from_z, last, from_last,
     bias_halves, bias_sent, bias_in, bias_sum, partial, partial_in,
     local_sem, send_sem, recv_sem,
 ):
     y, z_lo, z_hi, core, x = place()
-    z = z_hi * 2 + z_lo
     y_peers = [device((y + d) % 4, z_lo, z_hi, core, x) for d in (1, 2, 3)]
     x_peers = [device(y, z_lo, z_hi, core, (x + d) % 4) for d in (1, 2, 3)]
-    z_peers = [device(y, (z + d) % 2, ((z + d) % 8) // 2, core, x) for d in range(1, 8)]
+    z_peers = [device(y, z_lo, (z_hi + d) % 4, core, x) for d in (1, 2, 3)]
+    pair_peers = [device((y + d) % 4, 1 - z_lo, z_hi, core, x) for d in range(4)]
     partner = device(y, z_lo, z_hi, 1 - core, x)
     y_next, y_back, x_next, x_back = y_peers[0], y_peers[2], x_peers[0], x_peers[2]
-    peers = y_peers + x_peers + z_peers + [partner]
+    peers = y_peers + x_peers + z_peers + pair_peers + [partner]
     greet(peers)
 
     load_acts = pltpu.make_async_copy(acts_hbm, acts_ref, local_sem.at[0])
@@ -461,49 +461,48 @@
         store_grads(1, half, both[:, 0:768])
         store_grads(2, half, both[:, 768:1536])
 
-    def both_cores(f, w, k):
-        c = (x + f) % 4
+    first_next, first_back = (y_next, x_next), (y_back, x_back)
+    second_next, second_back = (x_next, y_next), (x_back, y_back)
+
+    def both_cores(half, a, b, n):
+        w = (y + (a, b)[half]) % 4
+        c = (x + (b, a)[half]) % 4
+        k = 2 * half + n
         return g_ref[w, k, core, c].astype(F32) + from_core[w, k, c].astype(F32)
 
     far, near = {}, {}
 
-    def start_chunk(half, f):
-        if f == 2:
+    def start_chunk(half, b):
+        if b == 2:
             for w in range(4):
                 core_copies[w, half].wait_recv()
-        for k in (2 * half, 2 * half + 1):
-            to_far[f, k] = both_cores(f, (y + 2) % 4, k).astype(BF16)
-        far[half, f] = (
-            send(to_far.at[f, 2 * half], from_far.at[0, half, f], y_next),
-            send(to_far.at[f, 2 * half + 1], from_far.at[1, half, f], y_back),
-        )
-
-    def pass_chunk(half, f):
-        up, down = (y + 1) % 4, (y + 3) % 4
-        one, two = 2 * half, 2 * half + 1
-        to_y[0, half, f, 1] = both_cores(f, up, two).astype(BF16)
-        to_y[1, half, f, 0] = both_cores(f, down, one).astype(BF16)
-        far[half, f][0].wait_recv()
-        to_y[0, half, f, 0] = (
-            both_cores(f, up, one) + from_far[0, half, f].astype(F32)
+        for n in range(2):
+            to_far[b, 2 * half + n] = both_cores(half, 2, b, n).astype(BF16)
+        far[half, b] = (
+            send(to_far.at[b, 2 * half], from_far.at[0, half, b], first_next[half]),
+            send(to_far.at[b, 2 * half + 1], from_far.at[1, half, b], first_back[half]),
+        )
+
+    def pass_chunk(half, b):
+        to_y[0, half, b, 1] = both_cores(half, 1, b, 1).astype(BF16)
+        to_y[1, half, b, 0] = both_cores(half, 3, b, 0).astype(BF16)
+        far[half, b][0].wait_recv()
+        to_y[0, half, b, 0] = (
+            both_cores(half, 1, b, 0) + from_far[0, half, b].astype(F32)
         ).astype(BF16)
-        up_copy = send(to_y.at[0, half, f], from_y.at[0, half, f], y_next)
-        far[half, f][1].wait_recv()
-        to_y[1, half, f, 1] = (
-            both_cores(f, down, two) + from_far[1, half, f].astype(F32)
+        up = send(to_y.at[0, half, b], from_y.at[0, half, b], first_next[half])
+        far[half, b][1].wait_recv()
+        to_y[1, half, b, 1] = (
+            both_cores(half, 3, b, 1) + from_far[1, half, b].astype(F32)
         ).astype(BF16)
-        near[half, f] = (up_copy, send(to_y.at[1, half, f], from_y.at[1, half, f], y_back))
+        down = send(to_y.at[1, half, b], from_y.at[1, half, b], first_back[half])
+        near[half, b] = (up, down)
 
     own_products(0)
     all_products(0)
     own_products(1)
     start_chunk(0, 2)
     start_chunk(0, 1)
-    all_products(1)
-    pass_chunk(0, 2)
-    start_chunk(0, 3)
-    pass_chunk(0, 1)
-    start_chunk(0, 0)
     for copy in bias_far:
         copy.wait_recv()
 
@@ -524,15 +523,20 @@
         send(bias_sent.at[0], bias_in.at[0], x_next),
         send(bias_sent.at[1], bias_in.at[1], x_back),
     ]
+    all_products(1)
+    pass_chunk(0, 2)
+    start_chunk(1, 2)
+    start_chunk(0, 3)
+    pass_chunk(0, 1)
+    start_chunk(1, 1)
+    start_chunk(0, 0)
+    pass_chunk(1, 2)
     pass_chunk(0, 3)
-    pass_chunk(0, 0)
-    attended_ref[...] = jnp.dot(merged_heads, w_ref[3], preferred_element_type=F32).astype(BF16)
-    start_chunk(1, 2)
-    start_chunk(1, 1)
-    pass_chunk(1, 2)
     start_chunk(1, 3)
     pass_chunk(1, 1)
+    pass_chunk(0, 0)
     start_chunk(1, 0)
+    attended_ref[...] = jnp.dot(merged_heads, w_ref[3], preferred_element_type=F32).astype(BF16)
     pass_chunk(1, 3)
 
     for copy in bias_near:
@@ -559,8 +563,8 @@
     early = lax.fori_loop(0, 4, tile_rows, jnp.zeros((16, 128), F32))
     pass_chunk(1, 0)
     partial[0] = lax.fori_loop(4, 8, tile_rows, early)
-    stages = ([partner], y_peers, x_peers, z_peers)
-    starts = (0, 1, 4, 7)
+    stages = ([partner], y_peers, x_peers, z_peers, pair_peers[0:1])
+    starts = (0, 1, 4, 7, 10)
     in_flight = {}
 
     def start_stage(n):
@@ -574,106 +578,121 @@
         for d, copy in enumerate(in_flight[n]):
             copy.wait_recv()
             total = total + partial_in[starts[n] + d]
-        if n < 3:
+        if n < 4:
             partial[n + 1] = total
             start_stage(n + 1)
         else:
             bias_out_ref[...] = total.T
 
-    def all_planes(half, f, n):
+    def first_sum(half, b, n):
         return (
-            both_cores(f, y, 2 * half + n)
-            + from_y[0, half, f, n].astype(F32)
-            + from_y[1, half, f, n].astype(F32)
-        )
-
-    def wait_planes(half, f):
-        near[half, f][0].wait_recv()
-        near[half, f][1].wait_recv()
-
-    x_far, x_near = {}, {}
-
-    def start_column(half):
-        wait_planes(half, 2)
+            both_cores(half, 0, b, n)
+            + from_y[0, half, b, n].astype(F32)
+            + from_y[1, half, b, n].astype(F32)
+        )
+
+    def wait_first(half, b):
+        near[half, b][0].wait_recv()
+        near[half, b][1].wait_recv()
+
+    x_far, x_near, pair_copies = {}, {}, {}
+
+    def start_second(half):
+        wait_first(half, 2)
         for n in range(2):
-            to_x[2, half, n] = all_planes(half, 2, n).astype(BF16)
+            to_x[2, half, n] = first_sum(half, 2, n).astype(BF16)
         x_far[half] = (
-            send(to_x.at[2, half, 0], x_halves.at[0, half], x_next),
-            send(to_x.at[2, half, 1], x_halves.at[1, half], x_back),
-        )
-
-    def pass_column(half):
-        wait_planes(half, 1)
-        to_x[0, half, 1] = all_planes(half, 1, 1).astype(BF16)
+            send(to_x.at[2, half, 0], x_halves.at[0, half], second_next[half]),
+            send(to_x.at[2, half, 1], x_halves.at[1, half], second_back[half]),
+        )
+
+    def pass_second(half):
+        wait_first(half, 1)
+        to_x[0, half, 1] = first_sum(half, 1, 1).astype(BF16)
         x_far[half][0].wait_recv()
         to_x[0, half, 0] = (
-            all_planes(half, 1, 0) + x_halves[0, half].astype(F32)
+            first_sum(half, 1, 0) + x_halves[0, half].astype(F32)
         ).astype(BF16)
-        up = send(to_x.at[0, half], from_x.at[0, half], x_next)
-        wait_planes(half, 3)
-        to_x[1, half, 0] = all_planes(half, 3, 0).astype(BF16)
+        up = send(to_x.at[0, half], from_x.at[0, half], second_next[half])
+        wait_first(half, 3)
+        to_x[1, half, 0] = first_sum(half, 3, 0).astype(BF16)
         x_far[half][1].wait_recv()
         to_x[1, half, 1] = (
-            all_planes(half, 3, 1) + x_halves[1, half].astype(F32)
+            first_sum(half, 3, 1) + x_halves[1, half].astype(F32)
         ).astype(BF16)
-        x_near[half] = (up, send(to_x.at[1, half], from_x.at[1, half], x_back))
-
-    def end_column(half):
-        wait_planes(half, 0)
+        down = send(to_x.at[1, half], from_x.at[1, half], second_back[half])
+        x_near[half] = (up, down)
+
+    def end_second(half):
+        wait_first(half, 0)
         for copy in x_near[half]:
             copy.wait_recv()
         for n in range(2):
             total = (
-                all_planes(half, 0, n)
+                first_sum(half, 0, n)
                 + from_x[0, half, n].astype(F32)
                 + from_x[1, half, n].astype(F32)
             )
-            own_sum[2 * half + n] = total
-            to_z[2 * half + n] = total.astype(BF16)
+            for side in range(2):
+                lanes = total[:, side * 384 : side * 384 + 384]
+                own_sum[side, 2 * half + n] = lanes
+                to_pair[side, 2 * half + n] = lanes.astype(BF16)
+        part = slice(2 * half, 2 * half + 2)
+        pair_copies[half] = send(
+            to_pair.at[1 - z_lo, part], from_pair.at[part], pair_peers[0]
+        )
 
     start_stage(0)
-    start_column(0)
+    start_second(0)
+    start_second(1)
     end_stage(0)
-    pass_column(0)
+    pass_second(0)
+    pass_second(1)
     end_stage(1)
-    start_column(1)
-    pass_column(1)
-    end_column(0)
+    end_second(0)
+    end_second(1)
     end_stage(2)
-    end_column(1)
-    z_copies = []
-    for d in range(7):
-        target = ((z + 1 + d) % 8) // 2
-        z_copies.append(send(to_z.at[target], from_z.at[d], z_peers[d]))
+    for half in range(2):
+        pair_copies[half].wait_recv()
+        for k in (2 * half, 2 * half + 1):
+            total = own_sum[z_lo, k] + from_pair[k].astype(F32)
+            own_sum[z_lo, k] = total
+            to_z[k] = total.astype(BF16)
+    z_copies = [
+        send(to_z.at[(z_hi + 1 + d) % 4], from_z.at[d], z_peers[d]) for d in range(3)
+    ]
     end_stage(3)
-    total = own_sum[z_hi]
+    total = own_sum[z_lo, z_hi]
     for d, copy in enumerate(z_copies):
         copy.wait_recv()
         total = total + from_z[d].astype(F32)
     last[...] = total.astype(BF16)
-    last_copies = [send(last, from_last.at[d], y_peers[d]) for d in range(3)]
-    results[y] = total.astype(BF16).astype(F32)
+    last_copies = [
+        send(last, from_last.at[d], peer) for d, peer in enumerate(y_peers + pair_peers)
+    ]
+    results[y, z_lo] = total.astype(BF16).astype(F32)
+    end_stage(4)
     for d, copy in enumerate(last_copies):
         copy.wait_recv()
-        results[(y + 3 - d) % 4] = from_last[d].astype(F32)
-    for n, ref in enumerate((gq_ref, gk_ref, gv_ref, go_ref)):
-        ref[...] = results[n]
+        if d < 3:
+            results[(y + 3 - d) % 4, z_lo] = from_last[d].astype(F32)
+        else:
+            results[(y + 7 - d) % 4, 1 - z_lo] = from_last[d].astype(F32)
     out.finish()
 
 
 def attend(own, cot, valid, acts, weights, bias, normed):
     vmem = pl.BlockSpec(memory_space=pltpu.VMEM)
     any_space = pl.BlockSpec(memory_space=pl.ANY)
-    grads = jax.ShapeDtypeStruct((24, 768), F32)
     return pl.pallas_call(
         attention_kernel,
         out_shape=(
             jax.ShapeDtypeStruct((128, 768), BF16),
-            grads, grads, grads, grads,
+            jax.ShapeDtypeStruct((4, 2, 24, 384), F32),
             jax.ShapeDtypeStruct((128, 16), F32),
         ),
         in_specs=[vmem] * 3 + [any_space] * 4,
-        out_specs=[vmem] * 6,
+        out_specs=[vmem] * 3,
         scratch_shapes=[
             pltpu.VMEM((1024, 768), BF16),
             pltpu.VMEM((4, 768, 768), BF16),
@@ -704,18 +723,19 @@
             pltpu.VMEM((3, 2, 2, 24, 768), BF16),
             pltpu.VMEM((2, 2, 2, 24, 768), BF16),
             pltpu.VMEM((2, 2, 24, 768), BF16),
-            pltpu.VMEM((4, 24, 768), BF16),
-            pltpu.VMEM((7, 24, 768), BF16),
-            pltpu.VMEM((4, 24, 768), F32),
-            pltpu.VMEM((24, 768), BF16),
-            pltpu.VMEM((3, 24, 768), BF16),
-            pltpu.VMEM((4, 24, 768), F32),
+            pltpu.VMEM((2, 4, 24, 384), F32),
+            pltpu.VMEM((2, 4, 24, 384), BF16),
+            pltpu.VMEM((4, 24, 384), BF16),
+            pltpu.VMEM((4, 24, 384), BF16),
+            pltpu.VMEM((3, 24, 384), BF16),
+            pltpu.VMEM((24, 384), BF16),
+            pltpu.VMEM((7, 24, 384), BF16),
             pltpu.VMEM((2, 8, 64, 128), BF16),
             pltpu.VMEM((2, 16, 64, 128), BF16),
             pltpu.VMEM((2, 16, 64, 128), BF16),
             pltpu.VMEM((16, 64, 128), F32),
-            pltpu.VMEM((4, 16, 128), F32),
-            pltpu.VMEM((14, 16, 128), F32),
+            pltpu.VMEM((5, 16, 128), F32),
+            pltpu.VMEM((11, 16, 128), F32),
             pltpu.SemaphoreType.DMA((7,)),
             pltpu.SemaphoreType.DMA((76,)),
             pltpu.SemaphoreType.DMA((76,)),
@@ -725,6 +745,32 @@
         ),
         name="attend",
     )(own, cot, valid, acts, weights, bias, normed)
+
+
+def finish_kernel(
+    attended_in, results_in, bias_in, attended_ref, gq_ref, gk_ref, gv_ref, go_ref, bias_ref
+):
+    attended_ref[...] = attended_in[...]
+    for n, ref in enumerate((gq_ref, gk_ref, gv_ref, go_ref)):
+        ref[:, 0:384] = results_in[n, 0]
+        ref[:, 384:768] = results_in[n, 1]
+    bias_ref[...] = bias_in[...]
+
+
+def finish(attended, results, grad_bias):
+    vmem = pl.BlockSpec(memory_space=pltpu.VMEM)
+    grads = jax.ShapeDtypeStruct((24, 768), F32)
+    return pl.pallas_call(
+        finish_kernel,
+        out_shape=(
+            jax.ShapeDtypeStruct((128, 768), BF16),
+            grads, grads, grads, grads,
+            jax.ShapeDtypeStruct((128, 16), F32),
+        ),
+        in_specs=[vmem] * 3,
+        out_specs=[vmem] * 6,
+        name="finish",
+    )(attended, results, grad_bias)
 
 
 def per_device(
@@ -739,7 +785,7 @@
         pair_gain[None],
         pair_bias_weight.T,
     )
-    attended, grad_query, grad_key, grad_value, grad_out, grad_bias = attend(
+    summed = attend(
         own_acts.reshape(copies * own_count, features),
         out_cotangent[0].reshape(copies * own_count, features),
         key_valid,
@@ -748,6 +794,7 @@
         bias,
         normed,
     )
+    attended, grad_query, grad_key, grad_value, grad_out, grad_bias = finish(*summed)
     attended = attended.reshape(1, copies, own_count, features)
     return (attended, grad_query, grad_key, grad_value, grad_out, grad_bias)
 

time: 123 us -> 109 us (0.89)
  local copies, waits for them, and re-layouts: 9.21 us -> 1.51 us
  Pallas kernels: 113 us -> 106 us
    pallas_call x1, Pallas kernels: 70.8 us -> 62.6 us  [attend(): pl.pallas_call(attention_kernel, out_shape=(jax.ShapeDtypeStruct((128, 76...]
    unnamed x6 -> x1, local copies, waits for them, and re-layouts: 9.21 us -> 1.51 us
    pallas_call x0 -> x1, Pallas kernels: none -> 1.81 us  [finish(): pl.pallas_call(finish_kernel, out_shape=(jax.ShapeDtypeStruct((128, 768),...]
where the time goes in v5:
time: 109 us; the launch traced here: 108 us
  Pallas kernels  106 us (97%)
  local copies, waits for them, and re-layouts  1.51 us (1%)
    pallas_call x1, Pallas kernels, attend(): pl.pallas_call(attention_kernel, out_shape=(jax.ShapeDtypeStruct((128, 76...  62.6 us
    pallas_call x1, Pallas kernels, gather(): pl.pallas_call(gather_kernel, out_shape=(jax.ShapeDtypeStruct((4, 4, 2, 4...  41.8 us

profile of v5, /device:TPU:2, one launch (start us, length us, event | category | flops | bytes accessed | tf_op | source)
XLA Modules:
  0.0 108.4 jit_solution(6807778611966743551)
XLA Ops:
  0.6 41.8 %gather.1 = (bf16[4,4,2,4,24,768]{5,4,3,2,1,0:T(8,128)(2,1)}, bf16[2,8,64,768]{3,2,1,0:T(8,128)(2,1)}, f32[4,4,16,16,128]{4,3,2,1,0:T(8,128)}, bf16[64,128,128]{2,1,0:T(8,128)(2,1)}) custom-call(bf16[24,768]{1,0:T(8,128)(2,1)} %wq_ref.1, bf16[24,768]{1,0:T(8,128)(2,1)} %wk_ref.1, bf16[24,768]{1,0:T(8,128)(2,1)} %wv_ref.1, bf16[24,768]{1,0:T(8,128)(2,1)} %wo_ref.1, ...), custom_call_target="tpu_custom_call" | custom-call | tf_op jit(solution)/shard_map/gather/pallas_call | solution.py:257
  42.4 62.6 %attend.1 = (bf16[128,768]{1,0:T(8,128)(2,1)}, f32[4,2,24,384]{3,2,1,0:T(8,128)}, f32[128,16]{1,0:T(8,128)}) custom-call(bf16[128,768]{1,0:T(8,128)(2,1)} %bitcast.13, bf16[128,768]{1,0:T(8,128)(2,1)} %bitcast.14, s32[1,512]{1,0:T(1,128)} %valid_ref.1, bf16[1024,768]{1,0:T(8,128)(2,1)} %bitcast.11, bf16[4,768,768]{2,1,0:T(8,128)(2,1)} %bitcast.9, ...), custom_call_target="tpu_custom_call" | custom-call | tf_op jit(solution)/shard_map/attend/pallas_call | solution.py:687
  105.1 1.8 %finish.1 = (bf16[128,768]{1,0:T(8,128)(2,1)}, f32[24,768]{1,0:T(8,128)}, f32[24,768]{1,0:T(8,128)}, f32[24,768]{1,0:T(8,128)}, f32[24,768]{1,0:T(8,128)}, /*index=5*/f32[128,16]{1,0:T(8,128)}) custom-call(bf16[128,768]{1,0:T(8,128)(2,1)} %get-tuple-element.23.attended_in, f32[4,2,24,384]{3,2,1,0:T(8,128)} %get-tuple-element.24.results_in, ...), custom_call_target="tpu_custom_call" | custom-call | tf_op jit(solution)/shard_map/finish/pallas_call | solution.py:763
  106.9 1.5 %copy.16 = f32[128,16]{0,1:T(8,128)} copy(f32[128,16]{1,0:T(8,128)} %get-tuple-element.37) | data formatting | bytes 16384

commit v6 on v5

--- a/solution.py
+++ b/solution.py
@@ -84,7 +84,6 @@
     for load in loads:
         load.start()
     stores = []
-    await_greetings(peers)
 
     def normalize_rows(block):
         loads[block].wait()
@@ -119,6 +118,8 @@
     def rows(z_owner):
         return acts_full.at[:, (z_owner % 4) * 2 + core]
 
+    normalize_rows(0)
+    await_greetings(peers)
     out = Sender(send_sem, recv_sem)
     send = out.send
     first, second = slice(0, 2), slice(2, 4)
@@ -148,7 +149,6 @@
     acts_up = send(acts_ref, rows(z_hi), z_next)
     acts_down = send(acts_ref, rows(z_hi), z_back)
     core_copies = [send(acts_ref, rows(z_hi), partner)]
-    normalize_rows(0)
 
     def swap_planes(owner):
         own = line(y, owner)
@@ -175,6 +175,8 @@
         part = bias_block(x + 1, chunk, slice(8, 16))
         bias_far.append(send(part, part, x_back))
 
+    send_bias(0)
+    normalize_rows(1)
     own_w.wait()
     for copy in z_copies:
         copy.wait_recv()
@@ -182,9 +184,8 @@
     x_up = send(own, own, x_next)
     x_down = send(own, own, x_back)
     planes = [swap_planes(x)]
-    send_bias(0)
-    normalize_rows(1)
     send_bias(1)
+    normalize_rows(2)
     x_up.wait_recv()
     part = line(y, x + 3, first)
     x_far_up = send(part, part, x_next)
@@ -193,7 +194,6 @@
     x_far_down = send(part, part, x_back)
     planes.append(swap_planes(x + 3))
     planes.append(swap_planes(x + 1))
-    normalize_rows(2)
     send_bias(2)
     acts_up.wait_recv()
     part = acts_full.at[0, ((z_hi + 3) % 4) * 2 + core]
@@ -204,6 +204,8 @@
     core_copies.append(send(rows(z_hi + 3), rows(z_hi + 3), partner))
     core_copies.append(send(rows(z_hi + 1), rows(z_hi + 1), partner))
     relay_bias(0)
+    normalize_rows(3)
+    send_bias(3)
     x_far_up.wait_recv()
     x_far_down.wait_recv()
     planes.append(swap_planes(x + 2))
@@ -224,8 +226,6 @@
             core_copies.append(send(whole, whole, partner))
 
     relay_planes(0)
-    normalize_rows(3)
-    send_bias(3)
     own_bias = pltpu.make_async_copy(tile_bias, bias_full.at[:, x], local_sem.at[2])
     own_bias.start()
     relay_bias(1)
@@ -553,16 +553,21 @@
     load_normed.wait()
 
     def tile_rows(block, total):
-        for u in range(8):
-            i = block * 8 + u
-            total = total + jnp.dot(
-                bias_sum[:, i, :].astype(BF16), normed_ref[i], preferred_element_type=F32
-            )
-        return total
-
-    early = lax.fori_loop(0, 4, tile_rows, jnp.zeros((16, 128), F32))
+        rows = [bias_sum[:, block * 8 + u, :].astype(BF16) for u in range(8)]
+        tile = normed_ref[block * 8 : block * 8 + 8].reshape(1024, 128)
+        return total + jnp.dot(
+            jnp.concatenate(rows, axis=1), tile, preferred_element_type=F32
+        )
+
+    early = jnp.zeros((16, 128), F32)
+    for block in range(4):
+        early = tile_rows(block, early)
+    partial[0] = early
     pass_chunk(1, 0)
-    partial[0] = lax.fori_loop(4, 8, tile_rows, early)
+    late = partial[0]
+    for block in range(4, 8):
+        late = tile_rows(block, late)
+    partial[0] = late
     stages = ([partner], y_peers, x_peers, z_peers, pair_peers[0:1])
     starts = (0, 1, 4, 7, 10)
     in_flight = {}
@@ -582,7 +587,7 @@
             partial[n + 1] = total
             start_stage(n + 1)
         else:
-            bias_out_ref[...] = total.T
+            bias_out_ref[...] = total
 
     def first_sum(half, b, n):
         return (
@@ -689,7 +694,7 @@
         out_shape=(
             jax.ShapeDtypeStruct((128, 768), BF16),
             jax.ShapeDtypeStruct((4, 2, 24, 384), F32),
-            jax.ShapeDtypeStruct((128, 16), F32),
+            jax.ShapeDtypeStruct((16, 128), F32),
         ),
         in_specs=[vmem] * 3 + [any_space] * 4,
         out_specs=[vmem] * 3,
@@ -765,7 +770,7 @@
         out_shape=(
             jax.ShapeDtypeStruct((128, 768), BF16),
             grads, grads, grads, grads,
-            jax.ShapeDtypeStruct((128, 16), F32),
+            jax.ShapeDtypeStruct((16, 128), F32),
         ),
         in_specs=[vmem] * 3,
         out_specs=[vmem] * 6,
@@ -796,7 +801,7 @@
     )
     attended, grad_query, grad_key, grad_value, grad_out, grad_bias = finish(*summed)
     attended = attended.reshape(1, copies, own_count, features)
-    return (attended, grad_query, grad_key, grad_value, grad_out, grad_bias)
+    return (attended, grad_query, grad_key, grad_value, grad_out, grad_bias.T)
 
 
 def solution(mesh):

time: 109 us -> 106 us (0.972)
  local copies, waits for them, and re-layouts: 1.51 us -> 0 us
    pallas_call x1, Pallas kernels: 62.6 us -> 60.6 us  [attend(): pl.pallas_call(attention_kernel, out_shape=(jax.ShapeDtypeStruct((128, 76...]
    unnamed x1 -> x0, local copies, waits for them, and re-layouts: 1.51 us -> none
where the time goes in v6:
time: 106 us
  Pallas kernels  105 us (99%)
    pallas_call x1, Pallas kernels, attend(): pl.pallas_call(attention_kernel, out_shape=(jax.ShapeDtypeStruct((128, 76...  60.6 us
    pallas_call x1, Pallas kernels, gather(): pl.pallas_call(gather_kernel, out_shape=(jax.ShapeDtypeStruct((4, 4, 2, 4...  42.7 us

profile of v6, /device:TPU:2, one launch (start us, length us, event | category | flops | bytes accessed | tf_op | source)
XLA Modules:
  0.0 105.8 jit_solution(7419598752265264372)
XLA Ops:
  0.6 42.7 %gather.1 = (bf16[4,4,2,4,24,768]{5,4,3,2,1,0:T(8,128)(2,1)}, bf16[2,8,64,768]{3,2,1,0:T(8,128)(2,1)}, f32[4,4,16,16,128]{4,3,2,1,0:T(8,128)}, bf16[64,128,128]{2,1,0:T(8,128)(2,1)}) custom-call(bf16[24,768]{1,0:T(8,128)(2,1)} %wq_ref.1, bf16[24,768]{1,0:T(8,128)(2,1)} %wk_ref.1, bf16[24,768]{1,0:T(8,128)(2,1)} %wv_ref.1, bf16[24,768]{1,0:T(8,128)(2,1)} %wo_ref.1, ...), custom_call_target="tpu_custom_call" | custom-call | tf_op jit(solution)/shard_map/gather/pallas_call | solution.py:257
  43.4 60.6 %attend.1 = (bf16[128,768]{1,0:T(8,128)(2,1)}, f32[4,2,24,384]{3,2,1,0:T(8,128)}, f32[16,128]{1,0:T(8,128)}) custom-call(bf16[128,768]{1,0:T(8,128)(2,1)} %bitcast.14, bf16[128,768]{1,0:T(8,128)(2,1)} %bitcast.15, s32[1,512]{1,0:T(1,128)} %valid_ref.1, bf16[1024,768]{1,0:T(8,128)(2,1)} %bitcast.12, bf16[4,768,768]{2,1,0:T(8,128)(2,1)} %bitcast.10, ...), custom_call_target="tpu_custom_call" | custom-call | tf_op jit(solution)/shard_map/attend/pallas_call | solution.py:692
  104.0 1.8 %finish.1 = (bf16[128,768]{1,0:T(8,128)(2,1)}, f32[24,768]{1,0:T(8,128)}, f32[24,768]{1,0:T(8,128)}, f32[24,768]{1,0:T(8,128)}, f32[24,768]{1,0:T(8,128)}, /*index=5*/f32[16,128]{1,0:T(8,128)}) custom-call(bf16[128,768]{1,0:T(8,128)(2,1)} %get-tuple-element.23.attended_in, f32[4,2,24,384]{3,2,1,0:T(8,128)} %get-tuple-element.24.results_in, ...), custom_call_target="tpu_custom_call" | custom-call | tf_op jit(solution)/shard_map/finish/pallas_call | solution.py:768

commit v7 on v6

--- a/solution.py
+++ b/solution.py
@@ -146,8 +146,6 @@
     ]
     out.started.extend(z_copies)
     own_acts.start()
-    acts_up = send(acts_ref, rows(z_hi), z_next)
-    acts_down = send(acts_ref, rows(z_hi), z_back)
     core_copies = [send(acts_ref, rows(z_hi), partner)]
 
     def swap_planes(owner):
@@ -184,6 +182,8 @@
     x_up = send(own, own, x_next)
     x_down = send(own, own, x_back)
     planes = [swap_planes(x)]
+    acts_up = send(acts_ref, rows(z_hi), z_next)
+    acts_down = send(acts_ref, rows(z_hi), z_back)
     send_bias(1)
     normalize_rows(2)
     x_up.wait_recv()
@@ -295,7 +295,7 @@
     own_ref, cot_ref, valid_ref, acts_hbm, w_hbm, bias_hbm, normed_hbm,
     attended_ref, results, bias_out_ref,
     acts_ref, w_ref, bias_ref, normed_ref,
-    query, key, value, grad, attention, query_grad, key_grad, value_grad, bias_total,
+    query, key, value, grad, attention, query_grad, key_carry, value_carry, bias_total,
     scores, pulled, weights, probs_low, score_grad, joint, bias_grad,
     g_ref, from_core, to_far, from_far, to_y, from_y, to_x, from_x, x_halves,
     own_sum, to_pair, from_pair, to_z, from_z, last, from_last,
@@ -332,8 +332,6 @@
     bias_total[...] = jnp.zeros_like(bias_total)
     attention[...] = jnp.zeros_like(attention)
     query_grad[...] = jnp.zeros_like(query_grad)
-    key_grad[...] = jnp.zeros_like(key_grad)
-    value_grad[...] = jnp.zeros_like(value_grad)
     load_w[3].wait()
     grad[...] = lax.dot_general(
         cot, w_ref[3], (((1,), (1,)), ((), ())), preferred_element_type=F32
@@ -341,17 +339,17 @@
     load_w[0].wait()
     query[...] = jnp.dot(own, w_ref[0], preferred_element_type=F32).astype(BF16)
     load_acts.wait()
-    load_w[1].wait()
-    load_w[2].wait()
-
-    def project_rows(block, _):
-        rows = pl.ds(pl.multiple_of(block * 256, 256), 256)
-        part = acts_ref[rows, :]
-        key[rows, :] = jnp.dot(part, w_ref[1], preferred_element_type=F32).astype(BF16)
-        value[rows, :] = jnp.dot(part, w_ref[2], preferred_element_type=F32).astype(BF16)
-        return 0
-
-    lax.fori_loop(0, 4, project_rows, 0)
+    for w, target in ((1, key), (2, value)):
+        load_w[w].wait()
+
+        def project_rows(block, _, w=w, target=target):
+            rows = pl.ds(pl.multiple_of(block * 256, 256), 256)
+            target[rows, :] = jnp.dot(
+                acts_ref[rows, :], w_ref[w], preferred_element_type=F32
+            ).astype(BF16)
+            return 0
+
+        lax.fori_loop(0, 4, project_rows, 0)
     load_bias.wait()
     keep = valid_ref[...] == 1
 
@@ -414,14 +412,26 @@
             for n in range(count):
                 back_win = jnp.where(masks[n], back[n * 64 : n * 64 + 64], back_win)
             query_grad[q_rows, lanes] += back_win
-            key_grad[k_rows, lanes] += lax.dot_general(
+            key_win = lax.dot_general(
                 score_grad[stacked, :], q_stack, (((0,), (0,)), ((), ())),
                 preferred_element_type=F32,
             )
-            value_grad[k_rows, lanes] += lax.dot_general(
+            value_win = lax.dot_general(
                 probs_low[stacked, :], g_stack, (((0,), (0,)), ((), ())),
                 preferred_element_type=F32,
             )
+            key_left, key_right = key_win[:, 0:128], key_win[:, 128:256]
+            value_left, value_right = value_win[:, 0:128], value_win[:, 128:256]
+            if start % 384 == 0:
+                key_carry[...] = key_right
+                value_carry[...] = value_right
+            else:
+                key_left = key_carry[...] + key_left
+                value_left = value_carry[...] + value_left
+                joint[k_rows, start + 128 : start + 256] = (key_right * scaling).astype(BF16)
+                joint[k_rows, start + 896 : start + 1024] = value_right.astype(BF16)
+            joint[k_rows, start : start + 128] = (key_left * scaling).astype(BF16)
+            joint[k_rows, start + 768 : start + 896] = value_left.astype(BF16)
         return 0
 
     lax.fori_loop(0, 2, one_copy, 0)
@@ -439,8 +449,6 @@
 
     merged_heads = attention[...].astype(BF16)
     q_low = (query_grad[...] * scaling).astype(BF16)
-    joint[:, 0:768] = (key_grad[...] * scaling).astype(BF16)
-    joint[:, 768:1536] = value_grad[...].astype(BF16)
     core_copies = {}
 
     def store_grads(w, half, product):
@@ -709,8 +717,8 @@
             pltpu.VMEM((128, 768), BF16),
             pltpu.VMEM((128, 768), F32),
             pltpu.VMEM((128, 768), F32),
-            pltpu.VMEM((1024, 768), F32),
-            pltpu.VMEM((1024, 768), F32),
+            pltpu.VMEM((512, 128), F32),
+            pltpu.VMEM((512, 128), F32),
             pltpu.VMEM((16, 64, 512), F32),
             pltpu.VMEM((320, 512), F32),
             pltpu.VMEM((320, 512), F32),

time: 106 us -> 106 us (level)
  no operation moved by 1% of the time
where the time goes in v7:
time: 106 us
  Pallas kernels  105 us (99%)
    pallas_call x1, Pallas kernels, attend(): pl.pallas_call(attention_kernel, out_shape=(jax.ShapeDtypeStruct((128, 76...  61.3 us
    pallas_call x1, Pallas kernels, gather(): pl.pallas_call(gather_kernel, out_shape=(jax.ShapeDtypeStruct((4, 4, 2, 4...  41.9 us

profile of v7, /device:TPU:2, one launch (start us, length us, event | category | flops | bytes accessed | tf_op | source)
XLA Modules:
  0.0 105.6 jit_solution(16144713742843076149)
XLA Ops:
  0.6 41.9 %gather.1 = (bf16[4,4,2,4,24,768]{5,4,3,2,1,0:T(8,128)(2,1)}, bf16[2,8,64,768]{3,2,1,0:T(8,128)(2,1)}, f32[4,4,16,16,128]{4,3,2,1,0:T(8,128)}, bf16[64,128,128]{2,1,0:T(8,128)(2,1)}) custom-call(bf16[24,768]{1,0:T(8,128)(2,1)} %wq_ref.1, bf16[24,768]{1,0:T(8,128)(2,1)} %wk_ref.1, bf16[24,768]{1,0:T(8,128)(2,1)} %wv_ref.1, bf16[24,768]{1,0:T(8,128)(2,1)} %wo_ref.1, ...), custom_call_target="tpu_custom_call" | custom-call | tf_op jit(solution)/shard_map/gather/pallas_call | solution.py:257
  42.5 61.3 %attend.1 = (bf16[128,768]{1,0:T(8,128)(2,1)}, f32[4,2,24,384]{3,2,1,0:T(8,128)}, f32[16,128]{1,0:T(8,128)}) custom-call(bf16[128,768]{1,0:T(8,128)(2,1)} %bitcast.14, bf16[128,768]{1,0:T(8,128)(2,1)} %bitcast.15, s32[1,512]{1,0:T(1,128)} %valid_ref.1, bf16[1024,768]{1,0:T(8,128)(2,1)} %bitcast.12, bf16[4,768,768]{2,1,0:T(8,128)(2,1)} %bitcast.10, ...), custom_call_target="tpu_custom_call" | custom-call | tf_op jit(solution)/shard_map/attend/pallas_call | solution.py:700
  103.8 1.8 %finish.1 = (bf16[128,768]{1,0:T(8,128)(2,1)}, f32[24,768]{1,0:T(8,128)}, f32[24,768]{1,0:T(8,128)}, f32[24,768]{1,0:T(8,128)}, f32[24,768]{1,0:T(8,128)}, /*index=5*/f32[16,128]{1,0:T(8,128)}) custom-call(bf16[128,768]{1,0:T(8,128)(2,1)} %get-tuple-element.23.attended_in, f32[4,2,24,384]{3,2,1,0:T(8,128)} %get-tuple-element.24.results_in, ...), custom_call_target="tpu_custom_call" | custom-call | tf_op jit(solution)/shard_map/finish/pallas_call | solution.py:776

commit v8 on v7

--- a/solution.py
+++ b/solution.py
@@ -293,8 +293,8 @@
 
 def attention_kernel(
     own_ref, cot_ref, valid_ref, acts_hbm, w_hbm, bias_hbm, normed_hbm,
-    attended_ref, results, bias_out_ref,
-    acts_ref, w_ref, bias_ref, normed_ref,
+    attended_hbm, results, bias_out_ref,
+    attended_ref, acts_ref, w_ref, bias_ref, normed_ref,
     query, key, value, grad, attention, query_grad, key_carry, value_carry, bias_total,
     scores, pulled, weights, probs_low, score_grad, joint, bias_grad,
     g_ref, from_core, to_far, from_far, to_y, from_y, to_x, from_x, x_halves,
@@ -545,6 +545,8 @@
     pass_chunk(0, 0)
     start_chunk(1, 0)
     attended_ref[...] = jnp.dot(merged_heads, w_ref[3], preferred_element_type=F32).astype(BF16)
+    store_attended = pltpu.make_async_copy(attended_ref, attended_hbm, local_sem.at[7])
+    store_attended.start()
     pass_chunk(1, 3)
 
     for copy in bias_near:
@@ -572,10 +574,6 @@
         early = tile_rows(block, early)
     partial[0] = early
     pass_chunk(1, 0)
-    late = partial[0]
-    for block in range(4, 8):
-        late = tile_rows(block, late)
-    partial[0] = late
     stages = ([partner], y_peers, x_peers, z_peers, pair_peers[0:1])
     starts = (0, 1, 4, 7, 10)
     in_flight = {}
@@ -655,8 +653,12 @@
             to_pair.at[1 - z_lo, part], from_pair.at[part], pair_peers[0]
         )
 
+    start_second(0)
+    late = partial[0]
+    for block in range(4, 8):
+        late = tile_rows(block, late)
+    partial[0] = late
     start_stage(0)
-    start_second(0)
     start_second(1)
     end_stage(0)
     pass_second(0)
@@ -691,6 +693,7 @@
             results[(y + 3 - d) % 4, z_lo] = from_last[d].astype(F32)
         else:
             results[(y + 7 - d) % 4, 1 - z_lo] = from_last[d].astype(F32)
+    store_attended.wait()
     out.finish()
 
 
@@ -705,8 +708,9 @@
             jax.ShapeDtypeStruct((16, 128), F32),
         ),
         in_specs=[vmem] * 3 + [any_space] * 4,
-        out_specs=[vmem] * 3,
+        out_specs=[any_space, vmem, vmem],
         scratch_shapes=[
+            pltpu.VMEM((128, 768), BF16),
             pltpu.VMEM((1024, 768), BF16),
             pltpu.VMEM((4, 768, 768), BF16),
             pltpu.VMEM((4, 4, 16, 16, 128), F32),
@@ -749,7 +753,7 @@
             pltpu.VMEM((16, 64, 128), F32),
             pltpu.VMEM((5, 16, 128), F32),
             pltpu.VMEM((11, 16, 128), F32),
-            pltpu.SemaphoreType.DMA((7,)),
+            pltpu.SemaphoreType.DMA((8,)),
             pltpu.SemaphoreType.DMA((76,)),
             pltpu.SemaphoreType.DMA((76,)),
         ],
@@ -761,17 +765,24 @@
 
 
 def finish_kernel(
-    attended_in, results_in, bias_in, attended_ref, gq_ref, gk_ref, gv_ref, go_ref, bias_ref
+    attended_in, results_in, bias_in, attended_ref, gq_ref, gk_ref, gv_ref, go_ref, bias_ref, sem
 ):
-    attended_ref[...] = attended_in[...]
+    moves = [(attended_in, attended_ref), (bias_in, bias_ref)]
     for n, ref in enumerate((gq_ref, gk_ref, gv_ref, go_ref)):
-        ref[:, 0:384] = results_in[n, 0]
-        ref[:, 384:768] = results_in[n, 1]
-    bias_ref[...] = bias_in[...]
+        moves.append((results_in.at[n, 0], ref.at[:, 0:384]))
+        moves.append((results_in.at[n, 1], ref.at[:, 384:768]))
+    copies = [
+        pltpu.make_async_copy(source, target, sem.at[k])
+        for k, (source, target) in enumerate(moves)
+    ]
+    for copy in copies:
+        copy.start()
+    for copy in copies:
+        copy.wait()
 
 
 def finish(attended, results, grad_bias):
-    vmem = pl.BlockSpec(memory_space=pltpu.VMEM)
+    any_space = pl.BlockSpec(memory_space=pl.ANY)
     grads = jax.ShapeDtypeStruct((24, 768), F32)
     return pl.pallas_call(
         finish_kernel,
@@ -780,8 +791,9 @@
             grads, grads, grads, grads,
             jax.ShapeDtypeStruct((16, 128), F32),
         ),
-        in_specs=[vmem] * 3,
-        out_specs=[vmem] * 6,
+        in_specs=[any_space] * 3,
+        out_specs=[any_space] * 6,
+        scratch_shapes=[pltpu.SemaphoreType.DMA((10,))],
         name="finish",
     )(attended, results, grad_bias)
 

time: 106 us -> 120 us (1.13)
  Pallas kernels: 105 us -> 119 us
    pallas_call x1, Pallas kernels: 1.8 us -> 16.3 us  [finish(): pl.pallas_call(finish_kernel, out_shape=(jax.ShapeDtypeStruct((128, 768),...]
where the time goes in v8:
time: 120 us
  Pallas kernels  119 us (99%)
    pallas_call x1, Pallas kernels, attend(): pl.pallas_call(attention_kernel, out_shape=(jax.ShapeDtypeStruct((128, 76...  61.3 us
    pallas_call x1, Pallas kernels, gather(): pl.pallas_call(gather_kernel, out_shape=(jax.ShapeDtypeStruct((4, 4, 2, 4...  41.9 us
    pallas_call x1, Pallas kernels, finish(): pl.pallas_call(finish_kernel, out_shape=(jax.ShapeDtypeStruct((128, 768),...  16.3 us

profile of v8, /device:TPU:2, one launch (start us, length us, event | category | flops | bytes accessed | tf_op | source)
XLA Modules:
  0.0 120.1 jit_solution(2513497609875218505)
XLA Ops:
  0.6 41.9 %gather.1 = (bf16[4,4,2,4,24,768]{5,4,3,2,1,0:T(8,128)(2,1)}, bf16[2,8,64,768]{3,2,1,0:T(8,128)(2,1)}, f32[4,4,16,16,128]{4,3,2,1,0:T(8,128)}, bf16[64,128,128]{2,1,0:T(8,128)(2,1)}) custom-call(bf16[24,768]{1,0:T(8,128)(2,1)} %wq_ref.1, bf16[24,768]{1,0:T(8,128)(2,1)} %wk_ref.1, bf16[24,768]{1,0:T(8,128)(2,1)} %wv_ref.1, bf16[24,768]{1,0:T(8,128)(2,1)} %wo_ref.1, ...), custom_call_target="tpu_custom_call" | custom-call | tf_op jit(solution)/shard_map/gather/pallas_call | solution.py:257
  42.5 61.3 %attend.1 = (bf16[128,768]{1,0:T(8,128)(2,1)}, f32[4,2,24,384]{3,2,1,0:T(8,128)}, f32[16,128]{1,0:T(8,128)}) custom-call(bf16[128,768]{1,0:T(8,128)(2,1)} %bitcast.14, bf16[128,768]{1,0:T(8,128)(2,1)} %bitcast.15, s32[1,512]{1,0:T(1,128)} %valid_ref.1, bf16[1024,768]{1,0:T(8,128)(2,1)} %bitcast.12, bf16[4,768,768]{2,1,0:T(8,128)(2,1)} %bitcast.10, ...), custom_call_target="tpu_custom_call" | custom-call | tf_op jit(solution)/shard_map/attend/pallas_call | solution.py:703
  103.8 16.3 %finish.1 = (bf16[128,768]{1,0:T(8,128)(2,1)}, f32[24,768]{1,0:T(8,128)}, f32[24,768]{1,0:T(8,128)}, f32[24,768]{1,0:T(8,128)}, f32[24,768]{1,0:T(8,128)}, /*index=5*/f32[16,128]{1,0:T(8,128)}) custom-call(bf16[128,768]{1,0:T(8,128)(2,1)} %get-tuple-element.23.attended_in, f32[4,2,24,384]{3,2,1,0:T(8,128)} %get-tuple-element.24.results_in, ...), custom_call_target="tpu_custom_call" | custom-call | tf_op jit(solution)/shard_map/finish/pallas_call | solution.py:787

commit v9 on v7

--- a/solution.py
+++ b/solution.py
@@ -262,7 +262,7 @@
             jax.ShapeDtypeStruct((4, 4, 16, 16, 128), F32),
             jax.ShapeDtypeStruct((64, 128, 128), BF16),
         ),
-        in_specs=[any_space] * 6 + [vmem] * 2,
+        in_specs=[vmem] * 5 + [any_space] + [vmem] * 2,
         out_specs=[any_space] * 4,
         scratch_shapes=[
             pltpu.VMEM((4, 16, 16, 128), F32),

time: 106 us -> 107 us (level)
  no operation moved by 1% of the time
where the time goes in v9:
time: 107 us; the launch traced here: 106 us
  Pallas kernels  106 us (99%)
    pallas_call x1, Pallas kernels, attend(): pl.pallas_call(attention_kernel, out_shape=(jax.ShapeDtypeStruct((128, 76...  62 us
    pallas_call x1, Pallas kernels, gather(): pl.pallas_call(gather_kernel, out_shape=(jax.ShapeDtypeStruct((4, 4, 2, 4...  41.7 us

profile of v9, /device:TPU:2, one launch (start us, length us, event | category | flops | bytes accessed | tf_op | source)
XLA Modules:
  0.0 106.2 jit_solution(16216892509203299293)
XLA Ops:
  0.6 41.7 %gather.1 = (bf16[4,4,2,4,24,768]{5,4,3,2,1,0:T(8,128)(2,1)}, bf16[2,8,64,768]{3,2,1,0:T(8,128)(2,1)}, f32[4,4,16,16,128]{4,3,2,1,0:T(8,128)}, bf16[64,128,128]{2,1,0:T(8,128)(2,1)}) custom-call(bf16[24,768]{1,0:T(8,128)(2,1)} %wq_ref.1, bf16[24,768]{1,0:T(8,128)(2,1)} %wk_ref.1, bf16[24,768]{1,0:T(8,128)(2,1)} %wv_ref.1, bf16[24,768]{1,0:T(8,128)(2,1)} %wo_ref.1, ...), custom_call_target="tpu_custom_call" | custom-call | tf_op jit(solution)/shard_map/gather/pallas_call | solution.py:257
  42.4 62.0 %attend.1 = (bf16[128,768]{1,0:T(8,128)(2,1)}, f32[4,2,24,384]{3,2,1,0:T(8,128)}, f32[16,128]{1,0:T(8,128)}) custom-call(bf16[128,768]{1,0:T(8,128)(2,1)} %bitcast.14, bf16[128,768]{1,0:T(8,128)(2,1)} %bitcast.15, s32[1,512]{1,0:T(1,128)} %valid_ref.1, bf16[1024,768]{1,0:T(8,128)(2,1)} %bitcast.12, bf16[4,768,768]{2,1,0:T(8,128)(2,1)} %bitcast.10, ...), custom_call_target="tpu_custom_call" | custom-call | tf_op jit(solution)/shard_map/attend/pallas_call | solution.py:700
  104.4 1.8 %finish.1 = (bf16[128,768]{1,0:T(8,128)(2,1)}, f32[24,768]{1,0:T(8,128)}, f32[24,768]{1,0:T(8,128)}, f32[24,768]{1,0:T(8,128)}, f32[24,768]{1,0:T(8,128)}, /*index=5*/f32[16,128]{1,0:T(8,128)}) custom-call(bf16[128,768]{1,0:T(8,128)(2,1)} %get-tuple-element.23.attended_in, f32[4,2,24,384]{3,2,1,0:T(8,128)} %get-tuple-element.24.results_in, ...), custom_call_target="tpu_custom_call" | custom-call | tf_op jit(solution)/shard_map/finish/pallas_call | solution.py:776
